TPU v7x, 512 devices: a whole 4x8x8 slice. The times are simulated.
512 devices in a mesh: section: 32 (over x, z_lo, core), tile: 16 (over z_hi, y).
Axes of the slice: x: 4, y: 8, z: 8 (z_hi: 2, z_lo: 4; z = z_hi * 4 + z_lo), core: 2. Of those that a mesh axis runs over, the one named last changes fastest.
Arguments:
- saved_inputs: bfloat16 [32, 4, 256, 32, 256], P('section', None, 'tile'), may hold values from -6 to 6
- relu_mask: int32 [32, 4, 256, 32, 256], P('section', None, 'tile'), may hold values from 0 to 1
- grads_in: bfloat16 [32, 256, 32, 256], P('section', 'tile'), may hold values from -6 to 6
- head_grads: bfloat16 [3, 256, 32, 256], P(None, 'tile'), may hold values from -6 to 6
- kernels: bfloat16 [32, 3, 3, 256, 256], P('section'), may hold values from -0.125 to 0.125
- bn_scale: float32 [32, 256], P('section'), may hold values from 0.5 to 2
Outputs:
- kernel_grads: float32 [32, 2304, 256], P('section', 'tile')
- outgoing: bfloat16 [32, 256, 32, 256], P('section', 'tile')
All inputs are finite; a program needn't handle non-finite values.
Results may differ from a plain program's by a relative error of at most 0.019.
Values may be sent and summed in bfloat16 or wider, within the bound.
A program may use at most 64 MiB of HBM per device.

v0:
```python
import math

import jax
import jax.numpy as jnp
from jax import lax
from jax.sharding import PartitionSpec as P


def with_halo(shard, sides, width):
    for axis, dim in sides:
        count, length = (lax.axis_size(axis), shard.shape[dim])
        up = [(i, (i + 1) % count) for i in range(count - 1)]
        down = [(j, i) for i, j in up]
        last = lax.slice_in_dim(shard, length - width, length, axis=dim)
        leading = lax.slice_in_dim(shard, 0, width, axis=dim)
        before = lax.ppermute(last, axis, up)
        after = lax.ppermute(leading, axis, down)
        shard = jnp.concatenate([before, shard, after], axis=dim)
    return shard


def shifted(block, axis, distance):
    devices = range(lax.axis_size(axis))
    route = [(i - distance, i) for i in devices if i - distance in devices]
    return lax.ppermute(block, axis, route)


def windows(padded, height, columns):
    pieces = [padded[a : a + height, b : b + columns] for a in range(3) for b in range(3)]
    joined = jnp.concatenate(pieces, axis=-1)
    return joined.reshape(height * columns, -1)


def sum_kernels(patch_list, grad_list):
    all_patches = jnp.concatenate(patch_list, axis=0)
    all_grads = jnp.concatenate(grad_list, axis=0)
    return lax.psum_scatter(
        lax.dot_general(
            all_patches, all_grads, (((0,), (0,)), ((), ())), preferred_element_type=jnp.float32
        ).astype(jnp.bfloat16),
        "tile",
        scatter_dimension=0,
        tiled=True,
    ).astype(jnp.float32)


def per_device(saved_inputs, relu_mask, grads_in, head_grads, kernels, bn_scale):
    inputs = saved_inputs[0]
    gate_bits = relu_mask[0]
    kernel = kernels[0]
    scales = bn_scale[0]
    tick_count, height, columns, channels = inputs.shape
    flipped = kernel[::-1, ::-1].transpose(0, 1, 3, 2).reshape(9 * channels, channels)
    top_section = lax.axis_index("section") == lax.axis_size("section") - 1
    gradient = grads_in[0]
    patch_list = []
    grad_list = []
    back_grad = gradient
    kernel_total = None
    for tick in range(tick_count):
        framed = with_halo(inputs[tick], (("tile", 0),), 1)
        padded_in = jnp.pad(framed, ((0, 0), (1, 1), (0, 0)))
        patch_list.append(windows(padded_in, height, columns))
        pre_grad = (
            gradient.astype(jnp.float32) * gate_bits[tick].astype(jnp.float32) * scales
        ).astype(jnp.bfloat16)
        grad_list.append(pre_grad.reshape(-1, channels))
        framed_grad = with_halo(pre_grad, (("tile", 0),), 1)
        padded_grad = jnp.pad(framed_grad, ((0, 0), (1, 1), (0, 0)))
        summed = jnp.dot(
            windows(padded_grad, height, columns), flipped, preferred_element_type=jnp.float32
        )
        summed = summed.reshape(height, columns, channels)
        back_grad = summed.astype(jnp.bfloat16)
        if tick + 1 < tick_count:
            received = shifted(back_grad, "section", -1)
            gradient = jnp.where(top_section, head_grads[tick], received)
    kernel_total = sum_kernels(patch_list, grad_list)
    divisor = math.sqrt(tick_count * height * lax.axis_size("tile") * columns)
    return ((kernel_total / divisor)[None], back_grad[None])


def solution(mesh):
    return jax.shard_map(
        per_device,
        mesh=mesh,
        in_specs=(
            P("section", None, "tile", None, None),
            P("section", None, "tile", None, None),
            P("section", "tile", None, None),
            P(None, "tile", None, None),
            P("section", None, None, None, None),
            P("section", None),
        ),
        out_specs=(P("section", "tile", None), P("section", "tile", None, None)),
        check_vma=False,
    )
```

profile of v0, /device:TPU:1, one launch (start us, length us, event | category | flops | bytes accessed | tf_op | source)
XLA Modules:
  0.0 377.3 jit_solution(3564633309787603179)
XLA Ops:
  7.2 1.4 fusion.27
  8.6 0.6 fusion.47
  9.2 4.6 %collective-permute-start.8 = (bf16[1,32,256]{2,1,0:T(8,128)(2,1)}, bf16[1,32,256]{2,1,0:T(8,128)(2,1)}, u32[]{:S(2)}, u32[]{:S(2)}) collective-permute-start(bf16[1,32,256]{2,1,0:T(8,128)(2,1)} %get-tuple-element.48), channel_id=1, source_target_pairs={{0,1},{1,2},{2,3},{3,4},{4,5},{5,6},{6,7},{7,8},{8,9},{9,10},{10,1... | collective-permute-start | bytes 49160 | tf_op jit(solution)/shard_map/ppermute | solution.py:16
  13.8 1.3 collective-permute-start.9
  15.1 1.5 slice_bitcast_fusion.7
  16.6 4.0 %collective-permute-start = (bf16[1,32,256]{2,1,0:T(8,128)(2,1)}, bf16[1,32,256]{2,1,0:T(8,128)(2,1)S(1)}, u32[]{:S(2)}, u32[]{:S(2)}) collective-permute-start(bf16[1,32,256]{2,1,0:T(8,128)(2,1)} %get-tuple-element.10), channel_id=1, source_target_pairs={{0,1},{1,2},{2,3},{3,4},{4,5},{5,6},{6,7},{7,8},{8,9},{9,10},{10,1... | collective-permute-start | bytes 49160 | tf_op jit(solution)/shard_map/ppermute | solution.py:16
  20.6 1.3 collective-permute-start.1
  21.9 4.6 %collective-permute-start.2 = (bf16[1,32,256]{2,1,0:T(8,128)(2,1)}, bf16[1,32,256]{2,1,0:T(8,128)(2,1)}, u32[]{:S(2)}, u32[]{:S(2)}) collective-permute-start(bf16[1,32,256]{2,1,0:T(8,128)(2,1)} %get-tuple-element.15), channel_id=1, source_target_pairs={{0,1},{1,2},{2,3},{3,4},{4,5},{5,6},{6,7},{7,8},{8,9},{9,10},{10,1... | collective-permute-start | bytes 49160 | tf_op jit(solution)/shard_map/ppermute | solution.py:16
  26.5 2.6 fusion.39
  29.1 0.8 fusion.29
  29.9 1.6 copy.8
  31.5 1.1 rev.3
  32.6 1.3 collective-permute-start.3
  33.9 4.0 %collective-permute-start.4 = (bf16[1,32,256]{2,1,0:T(8,128)(2,1)}, bf16[1,32,256]{2,1,0:T(8,128)(2,1)S(1)}, u32[]{:S(2)}, u32[]{:S(2)}) collective-permute-start(bf16[1,32,256]{2,1,0:T(8,128)(2,1)} %get-tuple-element.13), channel_id=1, source_target_pairs={{0,1},{1,2},{2,3},{3,4},{4,5},{5,6},{6,7},{7,8},{8,9},{9,10},{10,1... | collective-permute-start | bytes 49160 | tf_op jit(solution)/shard_map/ppermute | solution.py:16
  37.9 0.9 select_maximum_fusion.6
  38.8 0.8 fusion.37
  39.9 0.7 fusion.36
  40.8 0.8 convolution_convert_fusion.3
  41.6 1.3 collective-permute-start.5
  42.9 4.8 %collective-permute-start.6 = (bf16[1,32,256]{2,1,0:T(8,128)(2,1)S(1)}, bf16[1,32,256]{2,1,0:T(8,128)(2,1)S(1)}, u32[]{:S(2)}, u32[]{:S(2)}) collective-permute-start(bf16[1,32,256]{2,1,0:T(8,128)(2,1)S(1)} %copy-done.16), channel_id=1, source_target_pairs={{0,1},{1,2},{2,3},{3,4},{4,5},{5,6},{6,7},{7,8},{8,9},{9,10},{10,1... | collective-permute-start | bytes 49160 | tf_op jit(solution)/shard_map/ppermute | solution.py:16
  47.8 1.3 collective-permute-start.7
  49.1 7.5 %collective-permute-start.10 = (bf16[16,32,256]{2,1,0:T(8,128)(2,1)S(1)}, bf16[16,32,256]{2,1,0:T(8,128)(2,1)S(1)}, u32[]{:S(2)}, u32[]{:S(2)}) collective-permute-start(bf16[16,32,256]{2,1,0:T(8,128)(2,1)S(1)} %convolution_convert_fusion.3), channel_id=1, source_target_pairs={{16,0},{32,16},{48,32},{64,48},{80,64},{96,80},{112,96},{128,112},... | collective-permute-start | bytes 786440 | tf_op jit(solution)/shard_map/ppermute | solution.py:25
  56.6 1.1 select_maximum_fusion.12
  58.0 0.2 fusion.41
  58.3 0.6 copy-done.1
  59.0 0.4 select_maximum_fusion.8
  59.9 0.8 pad_maximum_fusion.12
  61.1 0.7 copy-done.9
  62.1 0.7 copy-done.8
  63.3 4.3 %collective-permute-start.11 = (bf16[1,32,256]{2,1,0:T(8,128)(2,1)S(1)}, bf16[1,32,256]{2,1,0:T(8,128)(2,1)S(1)}, u32[]{:S(2)}, u32[]{:S(2)}) collective-permute-start(bf16[1,32,256]{2,1,0:T(8,128)(2,1)S(1)} %get-tuple-element.46), channel_id=1, source_target_pairs={{0,1},{1,2},{2,3},{3,4},{4,5},{5,6},{6,7},{7,8},{8,9},{9,10},{10,1... | collective-permute-start | bytes 49160 | tf_op jit(solution)/shard_map/ppermute | solution.py:16
  67.6 1.3 collective-permute-start.12
  68.9 3.1 collective-permute-done.12
  72.6 0.8 convolution_convert_fusion.2
  73.4 3.1 collective-permute-start.13
  76.6 6.1 %collective-permute-done.13 = bf16[16,32,256]{2,1,0:T(8,128)(2,1)S(1)} collective-permute-done((bf16[16,32,256]{2,1,0:T(8,128)(2,1)S(1)}, bf16[16,32,256]{2,1,0:T(8,128)(2,1)S(1)}, u32[]{:S(2)}, u32[]{:S(2)}) %collective-permute-start.13) | collective-permute-done | bytes 262176 | tf_op jit(solution)/shard_map/ppermute | solution.py:25
  82.9 5.9 %collective-permute-start.14 = (bf16[1,32,256]{2,1,0:T(8,128)(2,1)S(1)}, bf16[1,32,256]{2,1,0:T(8,128)(2,1)S(1)}, u32[]{:S(2)}, u32[]{:S(2)}) collective-permute-start(bf16[1,32,256]{2,1,0:T(8,128)(2,1)S(1)} %get-tuple-element.44), channel_id=1, source_target_pairs={{0,1},{1,2},{2,3},{3,4},{4,5},{5,6},{6,7},{7,8},{8,9},{9,10},{10,1... | collective-permute-start | bytes 49160 | tf_op jit(solution)/shard_map/ppermute | solution.py:16
  88.8 1.3 collective-permute-start.15
  90.1 9.4 %collective-permute-done.15 = bf16[1,32,256]{2,1,0:T(8,128)(2,1)S(1)} collective-permute-done((bf16[1,32,256]{2,1,0:T(8,128)(2,1)S(1)}, bf16[1,32,256]{2,1,0:T(8,128)(2,1)S(1)}, u32[]{:S(2)}, u32[]{:S(2)}) %collective-permute-start.15) | collective-permute-done | bytes 16416 | tf_op jit(solution)/shard_map/ppermute | solution.py:17
  100.2 0.8 convolution_convert_fusion.1
  101.0 2.1 collective-permute-start.16
  103.1 6.0 %collective-permute-done.16 = bf16[16,32,256]{2,1,0:T(8,128)(2,1)S(1)} collective-permute-done((bf16[16,32,256]{2,1,0:T(8,128)(2,1)S(1)}, bf16[16,32,256]{2,1,0:T(8,128)(2,1)S(1)}, u32[]{:S(2)}, u32[]{:S(2)}) %collective-permute-start.16) | collective-permute-done | bytes 262176 | tf_op jit(solution)/shard_map/ppermute | solution.py:25
  109.3 3.9 %fusion.8 = bf16[2304,256]{1,0:T(8,128)(2,1)} fusion(bf16[512,2304]{1,0:T(8,128)(2,1)S(1)} %constant_dynamic-update-slice_fusion.27, bf16[512,2304]{1,0:T(8,128)(2,1)S(1)} %constant_dynamic-update-slice_fusion.18, bf16[512,2304]{1,0:T(8,128)(2,1)S(1)} %constant_dynamic-update-slice_fusion.9, bf16[512,2304]{1,0:T(8,128)(2,1)S(1)} %constant_dynamic-update-slice_fusion, ...), kind=kOutput, calls=%fused_computation.8 | convolution fusion | flops 2458451968 | bytes 11665408 | tf_op jit(solution)/shard_map/dot_general | solution.py:38
  113.2 9.3 %collective-permute-start.17 = (bf16[1,32,256]{2,1,0:T(8,128)(2,1)S(1)}, bf16[1,32,256]{2,1,0:T(8,128)(2,1)S(1)}, u32[]{:S(2)}, u32[]{:S(2)}) collective-permute-start(bf16[1,32,256]{2,1,0:T(8,128)(2,1)S(1)} %get-tuple-element.42), channel_id=1, source_target_pairs={{0,1},{1,2},{2,3},{3,4},{4,5},{5,6},{6,7},{7,8},{8,9},{9,10},{10,1... | collective-permute-start | bytes 49160 | tf_op jit(solution)/shard_map/ppermute | solution.py:16
  122.5 1.3 collective-permute-start.18
  123.8 9.5 %collective-permute-done.18 = bf16[1,32,256]{2,1,0:T(8,128)(2,1)S(1)} collective-permute-done((bf16[1,32,256]{2,1,0:T(8,128)(2,1)S(1)}, bf16[1,32,256]{2,1,0:T(8,128)(2,1)S(1)}, u32[]{:S(2)}, u32[]{:S(2)}) %collective-permute-start.18) | collective-permute-done | bytes 16416 | tf_op jit(solution)/shard_map/ppermute | solution.py:17
  133.8 1.5 fusion.11
  135.3 233.6 %reduce-scatter.2.cloned.1.call-done = bf16[144,256]{1,0:T(8,128)(2,1)} async-done(((bf16[2304,256]{1,0:T(8,128)(2,1)}), bf16[144,256]{1,0:T(8,128)(2,1)}) %reduce-scatter.2.cloned.1.call-update) | async-done | bytes 73744 | tf_op jit(solution)/shard_map/reduce_scatter | solution.py:37
  368.9 1.6 multiply_bitcast_fusion
  (133 shorter events, 4.3 us)
Async XLA Ops:
  7.2 21.9 %copy-start = (s32[1,4,16,32,256]{4,3,2,1,0:T(8,128)S(1)}, s32[1,4,16,32,256]{4,3,2,1,0:T(8,128)}, u32[]{:S(2)}) copy-start(s32[1,4,16,32,256]{4,3,2,1,0:T(8,128)} %param.7) | copy-start | bytes 6291460
  7.2 361.7 %reduce-scatter.2.cloned.1.call-start = ((), (), s32[]{:S(2)}) async-start(), calls=%async_computation.1 | async-start | bytes 1253376 | tf_op jit(solution)/shard_map/reduce_scatter | solution.py:37
  8.6 20.5 %copy-start.6 = (bf16[1,16,32,256]{3,2,1,0:T(8,128)(2,1)S(1)}, bf16[1,16,32,256]{3,2,1,0:T(8,128)(2,1)}, u32[]{:S(2)}) copy-start(bf16[1,16,32,256]{3,2,1,0:T(8,128)(2,1)} %param.8) | copy-start | bytes 786436
  8.6 20.5 %copy-start.13 = (f32[1,256]{1,0:T(1,128)S(1)}, f32[1,256]{1,0:T(1,128)}, u32[]{:S(2)}) copy-start(f32[1,256]{1,0:T(1,128)} %param.11) | copy-start | bytes 3076
  9.2 23.4 %collective-permute-start.8 = (bf16[1,32,256]{2,1,0:T(8,128)(2,1)}, bf16[1,32,256]{2,1,0:T(8,128)(2,1)}, u32[]{:S(2)}, u32[]{:S(2)}) collective-permute-start(bf16[1,32,256]{2,1,0:T(8,128)(2,1)} %get-tuple-element.48), channel_id=1, source_target_pairs={{0,1},{1,2},{2,3},{3,4},{4,5},{5,6},{6,7},{7,8},{8,9},{9,10},{10,1... | collective-permute-start | bytes 49160 | tf_op jit(solution)/shard_map/ppermute | solution.py:16
  13.8 20.1 %collective-permute-start.9 = (bf16[1,32,256]{2,1,0:T(8,128)(2,1)}, bf16[1,32,256]{2,1,0:T(8,128)(2,1)}, u32[]{:S(2)}, u32[]{:S(2)}) collective-permute-start(bf16[1,32,256]{2,1,0:T(8,128)(2,1)} %get-tuple-element.49), channel_id=1, source_target_pairs={{1,0},{2,1},{3,2},{4,3},{5,4},{6,5},{7,6},{8,7},{9,8},{10,9},{11,1... | collective-permute-start | bytes 49160 | tf_op jit(solution)/shard_map/ppermute | solution.py:17
  16.6 25.0 %collective-permute-start = (bf16[1,32,256]{2,1,0:T(8,128)(2,1)}, bf16[1,32,256]{2,1,0:T(8,128)(2,1)S(1)}, u32[]{:S(2)}, u32[]{:S(2)}) collective-permute-start(bf16[1,32,256]{2,1,0:T(8,128)(2,1)} %get-tuple-element.10), channel_id=1, source_target_pairs={{0,1},{1,2},{2,3},{3,4},{4,5},{5,6},{6,7},{7,8},{8,9},{9,10},{10,1... | collective-permute-start | bytes 49160 | tf_op jit(solution)/shard_map/ppermute | solution.py:16
  20.6 22.3 %collective-permute-start.1 = (bf16[1,32,256]{2,1,0:T(8,128)(2,1)}, bf16[1,32,256]{2,1,0:T(8,128)(2,1)}, u32[]{:S(2)}, u32[]{:S(2)}) collective-permute-start(bf16[1,32,256]{2,1,0:T(8,128)(2,1)} %get-tuple-element.16), channel_id=1, source_target_pairs={{1,0},{2,1},{3,2},{4,3},{5,4},{6,5},{7,6},{8,7},{9,8},{10,9},{11,1... | collective-permute-start | bytes 49160 | tf_op jit(solution)/shard_map/ppermute | solution.py:17
  21.9 25.8 %collective-permute-start.2 = (bf16[1,32,256]{2,1,0:T(8,128)(2,1)}, bf16[1,32,256]{2,1,0:T(8,128)(2,1)}, u32[]{:S(2)}, u32[]{:S(2)}) collective-permute-start(bf16[1,32,256]{2,1,0:T(8,128)(2,1)} %get-tuple-element.15), channel_id=1, source_target_pairs={{0,1},{1,2},{2,3},{3,4},{4,5},{5,6},{6,7},{7,8},{8,9},{9,10},{10,1... | collective-permute-start | bytes 49160 | tf_op jit(solution)/shard_map/ppermute | solution.py:16
  32.6 16.4 %collective-permute-start.3 = (bf16[1,32,256]{2,1,0:T(8,128)(2,1)}, bf16[1,32,256]{2,1,0:T(8,128)(2,1)S(1)}, u32[]{:S(2)}, u32[]{:S(2)}) collective-permute-start(bf16[1,32,256]{2,1,0:T(8,128)(2,1)} %get-tuple-element.14), channel_id=1, source_target_pairs={{1,0},{2,1},{3,2},{4,3},{5,4},{6,5},{7,6},{8,7},{9,8},{10,9},{11,1... | collective-permute-start | bytes 49160 | tf_op jit(solution)/shard_map/ppermute | solution.py:17
  33.9 24.4 %collective-permute-start.4 = (bf16[1,32,256]{2,1,0:T(8,128)(2,1)}, bf16[1,32,256]{2,1,0:T(8,128)(2,1)S(1)}, u32[]{:S(2)}, u32[]{:S(2)}) collective-permute-start(bf16[1,32,256]{2,1,0:T(8,128)(2,1)} %get-tuple-element.13), channel_id=1, source_target_pairs={{0,1},{1,2},{2,3},{3,4},{4,5},{5,6},{6,7},{7,8},{8,9},{9,10},{10,1... | collective-permute-start | bytes 49160 | tf_op jit(solution)/shard_map/ppermute | solution.py:16
  38.8 2.0 copy-start.5
  40.7 0.9 copy-start.17
  40.7 2.3 copy-start.16
  40.7 7.1 %copy-start.15 = (bf16[1,32,256]{2,1,0:T(8,128)(2,1)S(1)}, bf16[1,32,256]{2,1,0:T(8,128)(2,1)}, u32[]{:S(2)}) copy-start(bf16[1,32,256]{2,1,0:T(8,128)(2,1)} %get-tuple-element.17) | copy-start | bytes 49156
  40.7 15.9 %copy-start.3 = (bf16[16,32,256]{2,1,0:T(8,128)(2,1)S(1)}, bf16[16,32,256]{2,1,0:T(8,128)(2,1)}, u32[]{:S(2)}) copy-start(bf16[16,32,256]{2,1,0:T(8,128)(2,1)} %get-tuple-element.3) | copy-start | bytes 786436
  40.7 15.9 %copy-start.4 = (bf16[16,32,256]{2,1,0:T(8,128)(2,1)S(1)}, bf16[16,32,256]{2,1,0:T(8,128)(2,1)}, u32[]{:S(2)}) copy-start(bf16[16,32,256]{2,1,0:T(8,128)(2,1)} %get-tuple-element.4) | copy-start | bytes 786436
  41.6 16.7 %collective-permute-start.5 = (bf16[1,32,256]{2,1,0:T(8,128)(2,1)S(1)}, bf16[1,32,256]{2,1,0:T(8,128)(2,1)S(1)}, u32[]{:S(2)}, u32[]{:S(2)}) collective-permute-start(bf16[1,32,256]{2,1,0:T(8,128)(2,1)S(1)} %copy-done.17), channel_id=1, source_target_pairs={{1,0},{2,1},{3,2},{4,3},{5,4},{6,5},{7,6},{8,7},{9,8},{10,9},{11,1... | collective-permute-start | bytes 49160 | tf_op jit(solution)/shard_map/ppermute | solution.py:17
  42.9 15.4 %collective-permute-start.6 = (bf16[1,32,256]{2,1,0:T(8,128)(2,1)S(1)}, bf16[1,32,256]{2,1,0:T(8,128)(2,1)S(1)}, u32[]{:S(2)}, u32[]{:S(2)}) collective-permute-start(bf16[1,32,256]{2,1,0:T(8,128)(2,1)S(1)} %copy-done.16), channel_id=1, source_target_pairs={{0,1},{1,2},{2,3},{3,4},{4,5},{5,6},{6,7},{7,8},{8,9},{9,10},{10,1... | collective-permute-start | bytes 49160 | tf_op jit(solution)/shard_map/ppermute | solution.py:16
  47.8 10.6 %collective-permute-start.7 = (bf16[1,32,256]{2,1,0:T(8,128)(2,1)S(1)}, bf16[1,32,256]{2,1,0:T(8,128)(2,1)S(1)}, u32[]{:S(2)}, u32[]{:S(2)}) collective-permute-start(bf16[1,32,256]{2,1,0:T(8,128)(2,1)S(1)} %copy-done.15), channel_id=1, source_target_pairs={{1,0},{2,1},{3,2},{4,3},{5,4},{6,5},{7,6},{8,7},{9,8},{10,9},{11,1... | collective-permute-start | bytes 49160 | tf_op jit(solution)/shard_map/ppermute | solution.py:17
  49.1 13.8 %collective-permute-start.10 = (bf16[16,32,256]{2,1,0:T(8,128)(2,1)S(1)}, bf16[16,32,256]{2,1,0:T(8,128)(2,1)S(1)}, u32[]{:S(2)}, u32[]{:S(2)}) collective-permute-start(bf16[16,32,256]{2,1,0:T(8,128)(2,1)S(1)} %convolution_convert_fusion.3), channel_id=1, source_target_pairs={{16,0},{32,16},{48,32},{64,48},{80,64},{96,80},{112,96},{128,112},... | collective-permute-start | bytes 786440 | tf_op jit(solution)/shard_map/ppermute | solution.py:25
  58.0 1.0 copy-start.1
  58.0 1.0 copy-start.2
  59.9 1.0 copy-start.10
  60.8 1.0 copy-start.9
  61.8 1.0 copy-start.8
  62.0 1.2 copy-start.11
  62.0 1.1 copy-start.14
  63.3 5.6 %collective-permute-start.11 = (bf16[1,32,256]{2,1,0:T(8,128)(2,1)S(1)}, bf16[1,32,256]{2,1,0:T(8,128)(2,1)S(1)}, u32[]{:S(2)}, u32[]{:S(2)}) collective-permute-start(bf16[1,32,256]{2,1,0:T(8,128)(2,1)S(1)} %get-tuple-element.46), channel_id=1, source_target_pairs={{0,1},{1,2},{2,3},{3,4},{4,5},{5,6},{6,7},{7,8},{8,9},{9,10},{10,1... | collective-permute-start | bytes 49160 | tf_op jit(solution)/shard_map/ppermute | solution.py:16
  67.6 4.5 %collective-permute-start.12 = (bf16[1,32,256]{2,1,0:T(8,128)(2,1)S(1)}, bf16[1,32,256]{2,1,0:T(8,128)(2,1)S(1)}, u32[]{:S(2)}, u32[]{:S(2)}) collective-permute-start(bf16[1,32,256]{2,1,0:T(8,128)(2,1)S(1)} %get-tuple-element.47), channel_id=1, source_target_pairs={{1,0},{2,1},{3,2},{4,3},{5,4},{6,5},{7,6},{8,7},{9,8},{10,9},{11,1... | collective-permute-start | bytes 49160 | tf_op jit(solution)/shard_map/ppermute | solution.py:17
  72.6 4.0 %copy-start.7 = (bf16[1,1,16,32,256]{4,3,2,1,0:T(8,128)(2,1)S(1)}, bf16[1,1,16,32,256]{4,3,2,1,0:T(8,128)(2,1)}, u32[]{:S(2)}) copy-start(bf16[1,1,16,32,256]{4,3,2,1,0:T(8,128)(2,1)} %get-tuple-element.9) | copy-start | bytes 786436
  73.4 9.3 %collective-permute-start.13 = (bf16[16,32,256]{2,1,0:T(8,128)(2,1)S(1)}, bf16[16,32,256]{2,1,0:T(8,128)(2,1)S(1)}, u32[]{:S(2)}, u32[]{:S(2)}) collective-permute-start(bf16[16,32,256]{2,1,0:T(8,128)(2,1)S(1)} %convolution_convert_fusion.2), channel_id=1, source_target_pairs={{16,0},{32,16},{48,32},{64,48},{80,64},{96,80},{112,96},{128,112},... | collective-permute-start | bytes 786440 | tf_op jit(solution)/shard_map/ppermute | solution.py:25
  82.9 7.3 %collective-permute-start.14 = (bf16[1,32,256]{2,1,0:T(8,128)(2,1)S(1)}, bf16[1,32,256]{2,1,0:T(8,128)(2,1)S(1)}, u32[]{:S(2)}, u32[]{:S(2)}) collective-permute-start(bf16[1,32,256]{2,1,0:T(8,128)(2,1)S(1)} %get-tuple-element.44), channel_id=1, source_target_pairs={{0,1},{1,2},{2,3},{3,4},{4,5},{5,6},{6,7},{7,8},{8,9},{9,10},{10,1... | collective-permute-start | bytes 49160 | tf_op jit(solution)/shard_map/ppermute | solution.py:16
  88.8 10.8 %collective-permute-start.15 = (bf16[1,32,256]{2,1,0:T(8,128)(2,1)S(1)}, bf16[1,32,256]{2,1,0:T(8,128)(2,1)S(1)}, u32[]{:S(2)}, u32[]{:S(2)}) collective-permute-start(bf16[1,32,256]{2,1,0:T(8,128)(2,1)S(1)} %get-tuple-element.45), channel_id=1, source_target_pairs={{1,0},{2,1},{3,2},{4,3},{5,4},{6,5},{7,6},{8,7},{9,8},{10,9},{11,1... | collective-permute-start | bytes 49160 | tf_op jit(solution)/shard_map/ppermute | solution.py:17
  101.0 8.3 %copy-start.12 = (bf16[512,256]{1,0:T(8,128)(2,1)S(1)}, bf16[512,256]{1,0:T(8,128)(2,1)}, u32[]{:S(2)}) copy-start(bf16[512,256]{1,0:T(8,128)(2,1)} %fusion.29) | copy-start | bytes 786436
  101.0 8.2 %collective-permute-start.16 = (bf16[16,32,256]{2,1,0:T(8,128)(2,1)S(1)}, bf16[16,32,256]{2,1,0:T(8,128)(2,1)S(1)}, u32[]{:S(2)}, u32[]{:S(2)}) collective-permute-start(bf16[16,32,256]{2,1,0:T(8,128)(2,1)S(1)} %convolution_convert_fusion.1), channel_id=1, source_target_pairs={{16,0},{32,16},{48,32},{64,48},{80,64},{96,80},{112,96},{128,112},... | collective-permute-start | bytes 786440 | tf_op jit(solution)/shard_map/ppermute | solution.py:25
  113.2 10.6 %collective-permute-start.17 = (bf16[1,32,256]{2,1,0:T(8,128)(2,1)S(1)}, bf16[1,32,256]{2,1,0:T(8,128)(2,1)S(1)}, u32[]{:S(2)}, u32[]{:S(2)}) collective-permute-start(bf16[1,32,256]{2,1,0:T(8,128)(2,1)S(1)} %get-tuple-element.42), channel_id=1, source_target_pairs={{0,1},{1,2},{2,3},{3,4},{4,5},{5,6},{6,7},{7,8},{8,9},{9,10},{10,1... | collective-permute-start | bytes 49160 | tf_op jit(solution)/shard_map/ppermute | solution.py:16
  122.5 10.8 %collective-permute-start.18 = (bf16[1,32,256]{2,1,0:T(8,128)(2,1)S(1)}, bf16[1,32,256]{2,1,0:T(8,128)(2,1)S(1)}, u32[]{:S(2)}, u32[]{:S(2)}) collective-permute-start(bf16[1,32,256]{2,1,0:T(8,128)(2,1)S(1)} %get-tuple-element.43), channel_id=1, source_target_pairs={{1,0},{2,1},{3,2},{4,3},{5,4},{6,5},{7,6},{8,7},{9,8},{10,9},{11,1... | collective-permute-start | bytes 49160 | tf_op jit(solution)/shard_map/ppermute | solution.py:17
Sparse Core Ops, SparseCore 0:
  113.3 255.5 reduce-scatter.1
where the time goes:
time: 383 us; the launch traced here: 377 us
  waiting for transfers between devices  268 us (70%)
  starting transfers between devices  64.4 us (17%)
  between operations  15.1 us (4%)
  local copies, waits for them, and re-layouts  12.8 us (3%)
  other arithmetic  9.45 us (2%)
  matrix products  7.68 us (2%)
    reduce_scatter x1, waiting for transfers between devices, sum_kernels(): lax.psum_scatter(lax.dot_general(all_patches, all_grads, (((0,), (0,)), (...  234 us
    ppermute x8, starting transfers between devices, with_halo(): before = lax.ppermute(last, axis, up)  41.5 us
    ppermute x8, waiting for transfers between devices, with_halo(): after = lax.ppermute(leading, axis, down)  22.1 us
    ppermute x3, starting transfers between devices, shifted(): return lax.ppermute(block, axis, route)  12.6 us
    ppermute x3, waiting for transfers between devices, shifted(): return lax.ppermute(block, axis, route)  12.1 us
    ppermute x8, starting transfers between devices, with_halo(): after = lax.ppermute(leading, axis, down)  10.3 us
  transfers between devices with their start and end apart: 20, of which 6 were waited for; matrix products, arithmetic and copies ran while one was open for 5% of the time, Pallas kernels for 0%

commit v1 on v0

v1 whole, which is shorter than its diff:
```python
import functools
import math

import jax
import jax.numpy as jnp
from jax import lax
from jax.experimental import pallas as pl
from jax.experimental.pallas import tpu as pltpu
from jax.sharding import PartitionSpec as P

MESH = pl.DeviceIdType.MESH
F32 = jnp.float32
BF16 = jnp.bfloat16
T, H, W, C = 4, 16, 32, 256
PX = H * W
HALF = PX // 2
GRID = PX + 2 * W
SECTIONS, TILES, RING = 32, 16, 8
ROWS = 9 * C // TILES
MESSAGES = 2 * (RING - 1)
TN = (((0,), (0,)), ((), ()))
NT = (((1,), (1,)), ((), ()))


def loop(count, step, start=0):
    def one(i, carry):
        step(i)
        return carry

    lax.fori_loop(start, count, one, 0)


def kernel(
    x_hbm, m_hbm, gin_hbm, head_hbm, w_hbm, sc_hbm, kg_ref, out_ref,
    xv, mv, wv, sv, gb, pg, bg, acc, xt, edge_i, edge, mh, sbuf, rbuf, zs, zr,
    ld_x, ld_m, ld_w, ld_s, ld_e,
    gm_send, gm_recv, gh_send, gh_recv, hh_send, mh_send, mh_recv,
    rs_send, rs_recv, z_send, z_recv,
):
    s = lax.axis_index("section")
    j = lax.axis_index("tile")
    z, y = j // RING, j % RING
    up_ok, down_ok = j > 0, j < TILES - 1
    sends, takes = s > 0, s < SECTIONS - 1
    top = s == SECTIONS - 1

    def ring(distance):
        return z * RING + (y + distance + RING) % RING

    partner = (j + RING) % TILES

    barrier = pltpu.get_barrier_semaphore()

    def greet(section, tile):
        pl.semaphore_signal(barrier, inc=1, device_id=(section, tile), device_id_type=MESH)

    greet(s, ring(1))
    greet(s, ring(-1))
    greet(s, partner)
    pl.when(up_ok)(lambda: greet(s, j - 1))
    pl.when(down_ok)(lambda: greet(s, j + 1))

    @pl.when(takes)
    def _():
        greet(s + 1, j)
        pl.when(up_ok)(lambda: greet(s + 1, j - 1))
        pl.when(down_ok)(lambda: greet(s + 1, j + 1))

    def rows_of(h):
        return pl.ds(h * HALF, HALF)

    def edge_load(side):
        return pltpu.make_async_copy(
            m_hbm.at[:, pl.ds(side * (PX - W), W), :], edge_i.at[side], ld_e.at[side]
        )

    def first_load(h):
        return pltpu.make_async_copy(
            gin_hbm.at[rows_of(h)], gb.at[0, pl.ds(W + h * HALF, HALF)], gm_recv.at[0, h]
        )

    def head_load(t, h):
        return pltpu.make_async_copy(
            head_hbm.at[t, rows_of(h)], gb.at[t + 1, pl.ds(W + h * HALF, HALF)], gm_recv.at[t + 1, h]
        )

    def mask_load(t):
        return pltpu.make_async_copy(m_hbm.at[t], mv.at[t], ld_m.at[t])

    def x_load(t):
        return pltpu.make_async_copy(x_hbm.at[t], xv.at[t], ld_x.at[t])

    w_load = pltpu.make_async_copy(w_hbm, wv, ld_w)
    s_load = pltpu.make_async_copy(sc_hbm, sv, ld_s)
    edge_load(0).start()
    edge_load(1).start()
    s_load.start()
    first_load(0).start()
    first_load(1).start()
    mask_load(0).start()
    w_load.start()
    x_load(0).start()
    x_load(T - 1).start()
    for t in range(1, T):
        mask_load(t).start()
    for t in range(1, T - 1):
        x_load(t).start()

    @pl.when(top)
    def _():
        for t in range(T - 1):
            head_load(t, 0).start()
            head_load(t, 1).start()

    def clear(i):
        acc[pl.ds(pl.multiple_of(i * C, C), C), :] = jnp.zeros((C, C), F32)

    loop(9, clear)
    edge_load(0).wait()
    edge_load(1).wait()
    edge[...] = edge_i[...].astype(BF16)

    greeted = 3 + up_ok.astype(jnp.int32) + down_ok.astype(jnp.int32)
    greeted = greeted + jnp.where(sends, greeted - 2, 0)
    pl.semaphore_wait(barrier, greeted)

    def to_tile(src, dst, send, recv, section, tile):
        return pltpu.make_async_remote_copy(
            src_ref=src, dst_ref=dst, send_sem=send, recv_sem=recv,
            device_id=(section, tile), device_id_type=MESH,
        )

    def halo(t, side):
        return gb.at[t, pl.ds(side * (PX + W), W)]

    def edge_rows(side):
        return pl.ds(side * (PX - W), W)

    def first_edge(side):
        return to_tile(
            gin_hbm.at[edge_rows(side)], halo(0, 1 - side),
            gh_send.at[0, side], gh_recv.at[0, 1 - side], s, j - 1 + 2 * side,
        )

    def mask_edge(side):
        return to_tile(
            edge.at[side], mh.at[1 - side], mh_send.at[side], mh_recv.at[1 - side], s, j - 1 + 2 * side
        )

    def head_edge(t, side):
        return to_tile(
            head_hbm.at[t, edge_rows(side)], halo(t + 1, 1 - side),
            hh_send.at[t, side], gh_recv.at[t + 1, 1 - side], s, j - 1 + 2 * side,
        )

    def back_edge(t, side):
        return to_tile(
            bg.at[t, edge_rows(side)], halo(t + 1, 1 - side),
            gh_send.at[t + 1, side], gh_recv.at[t + 1, 1 - side], s - 1, j - 1 + 2 * side,
        )

    def back_half(t, h):
        return to_tile(
            bg.at[t, rows_of(h)], gb.at[t + 1, pl.ds(W + h * HALF, HALF)],
            gm_send.at[t, h], gm_recv.at[t + 1, h], s - 1, j,
        )

    has_tile = (up_ok, down_ok)

    for side in range(2):

        @pl.when(has_tile[side])
        def _(side=side):
            first_edge(side).start()
            mask_edge(side).start()

            @pl.when(top)
            def _():
                for t in range(T - 1):
                    head_edge(t, side).start()

    s_load.wait()
    scales = sv[...]

    def column_shifts(t, at, value):
        count = value.shape[0]
        column = lax.broadcasted_iota(jnp.int32, (count, C), 0) % W
        dst = pl.ds(at, count)
        right = jnp.where(column == W - 1, 0.0, pltpu.roll(value, count - 1, 0))
        left = jnp.where(column == 0, 0.0, pltpu.roll(value, 1, 0))
        pg[3 * t, dst, :] = right.astype(BF16)
        pg[3 * t + 1, dst, :] = value.astype(BF16)
        pg[3 * t + 2, dst, :] = left.astype(BF16)

    def pre_grad(t):
        mask_load(t).wait()
        for h in range(2):
            pltpu.make_async_copy(
                gin_hbm.at[rows_of(h)], gb.at[t, pl.ds(W + h * HALF, HALF)], gm_recv.at[t, h]
            ).wait()

        def main(h):
            at = pl.multiple_of(h * HALF, HALF)
            grads = gb[t, pl.ds(W + at, HALF), :].astype(F32)
            value = jnp.where(mv[t, pl.ds(at, HALF), :] != 0, grads * scales, 0.0)
            column_shifts(t, W + at, value)

        loop(2, main)
        for side in range(2):
            at = side * (PX + W)

            @pl.when(has_tile[side])
            def _(side=side, at=at):
                pltpu.make_async_copy(
                    gin_hbm.at[edge_rows(side)], halo(t, side), gh_recv.at[t, side]
                ).wait()
                grads = gb[t, pl.ds(at, W), :].astype(F32)
                value = grads * mh[side, t].astype(F32) * scales
                column_shifts(t, at, value)

            @pl.when(jnp.logical_not(has_tile[side]))
            def _(at=at):
                for b in range(3):
                    pg[3 * t + b, pl.ds(at, W), :] = jnp.zeros((W, C), BF16)

    def conv(t, at, count):
        total = None
        for a in range(3):
            rows = pl.ds(pl.multiple_of((2 - a) * W + at, W), count)
            for b in range(3):
                term = lax.dot_general(
                    pg[3 * t + b, rows, :], wv[(3 * a + b) * C : (3 * a + b + 1) * C, :],
                    NT, preferred_element_type=F32,
                )
                total = term if total is None else total + term
        return total.astype(BF16)

    def kernel_term(t):
        def one(a):
            rows = pl.ds(pl.multiple_of((2 - a) * W, W), PX)
            for b in range(3):
                dst = pl.ds(pl.multiple_of((3 * a + b) * C, C), C)
                acc[dst, :] += lax.dot_general(
                    xv[t], pg[3 * t + b, rows, :], TN, preferred_element_type=F32
                )

        loop(3, one)

    for side in range(2):

        @pl.when(has_tile[side])
        def _(side=side):
            pltpu.make_async_copy(edge.at[side], mh.at[side], mh_recv.at[side]).wait()

    w_load.wait()

    def tick(t):
        pre_grad(t)
        for h in range(2):
            bg[t, rows_of(h), :] = conv(t, h * HALF, HALF)

            @pl.when(sends)
            def _(h=h):
                pl.when(has_tile[h])(lambda: back_edge(t, h).start())
                back_half(t, h).start()

        x_load(t).wait()
        kernel_term(t)

    loop(T - 1, tick)

    x_load(T - 1).wait()
    turned = xv[T - 1].T
    xt[0:C, :] = turned
    xt[C : 2 * C, :] = turned

    last = T - 1
    pre_grad(last)

    def block_row(i):
        k = i + 2
        away = RING // 2 - k // 4
        near = jnp.logical_or(k % 4 == 0, k % 4 == 3)
        owner_y = (y + jnp.where(i % 2 == 0, away, -away) + RING) % RING
        owner_z = jnp.where(near, z, 1 - z)
        return owner_z * RING + owner_y

    def block_of(i):
        return pl.ds(pl.multiple_of(block_row(i) * ROWS, 16), ROWS)

    def message(i):
        return to_tile(
            sbuf.at[i], rbuf.at[i], rs_send.at[i], rs_recv.at[i], s, ring(1 - 2 * (i % 2))
        )

    def first_messages(i):
        row0 = block_row(i) * ROWS
        tap = row0 // C
        at = pl.multiple_of(row0 - tap * C, 16)
        lhs = xt[pl.ds(at, ROWS), :]

        def term(tap):
            a, b = tap // 3, tap % 3
            rows = pl.ds(pl.multiple_of((2 - a) * W, W), PX)
            return jnp.dot(lhs, pg[3 * last + b, rows, :], preferred_element_type=F32)

        row = lax.broadcasted_iota(jnp.int32, (ROWS, C), 0) + at
        own = jnp.where(row < C, term(tap), term(jnp.minimum(tap + 1, 8)))
        sbuf[i] = (acc[block_of(i), :] + own).astype(BF16)
        message(i).start()

    def pass_on(i):
        message(i - 4).wait_recv()
        sbuf[i] = (acc[block_of(i), :] + rbuf[i - 4].astype(F32)).astype(BF16)
        message(i).start()

    loop(4, first_messages)
    kernel_term(last)
    loop(8, pass_on, 4)
    out_ref[...] = conv(last, 0, PX)
    loop(MESSAGES, pass_on, 8)

    m = MESSAGES
    message(m - 3).wait_recv()
    message(m - 2).wait_recv()
    total = acc[block_of(m + 1), :] + rbuf[m - 3].astype(F32) + rbuf[m - 2].astype(F32)
    zs[...] = total.astype(BF16)
    across = to_tile(zs, zr, z_send, z_recv, s, partner)
    across.start()
    message(m - 4).wait_recv()
    message(m - 1).wait_recv()
    total = acc[block_of(m), :] + rbuf[m - 4].astype(F32) + rbuf[m - 1].astype(F32)
    across.wait_recv()
    kg_ref[...] = (total + zr[...].astype(F32)) * (1.0 / math.sqrt(T * TILES * PX))

    across.wait_send()
    loop(MESSAGES, lambda i: message(i).wait_send())
    for side in range(2):

        @pl.when(has_tile[side])
        def _(side=side):
            first_edge(side).wait_send()
            mask_edge(side).wait_send()

            @pl.when(top)
            def _():
                for t in range(T - 1):
                    head_edge(t, side).wait_send()

            @pl.when(sends)
            def _():
                for t in range(T - 1):
                    back_edge(t, side).wait_send()

    @pl.when(sends)
    def _():
        for t in range(T - 1):
            back_half(t, 0).wait_send()
            back_half(t, 1).wait_send()


def per_device(saved_inputs, relu_mask, grads_in, head_grads, kernels, bn_scale):
    any_space = pl.BlockSpec(memory_space=pl.ANY)
    vmem = pl.BlockSpec(memory_space=pltpu.VMEM)
    dma = pltpu.SemaphoreType.DMA
    kernel_grads, outgoing = pl.pallas_call(
        kernel,
        out_shape=(
            jax.ShapeDtypeStruct((ROWS, C), F32),
            jax.ShapeDtypeStruct((PX, C), BF16),
        ),
        in_specs=[any_space] * 6,
        out_specs=(vmem, vmem),
        scratch_shapes=[
            pltpu.VMEM((T, PX, C), BF16),
            pltpu.VMEM((T, PX, C), jnp.int32),
            pltpu.VMEM((9 * C, C), BF16),
            pltpu.VMEM((1, C), F32),
            pltpu.VMEM((T, GRID, C), BF16),
            pltpu.VMEM((3 * T, GRID, C), BF16),
            pltpu.VMEM((T - 1, PX, C), BF16),
            pltpu.VMEM((9 * C, C), F32),
            pltpu.VMEM((2 * C, PX), BF16),
            pltpu.VMEM((2, T, W, C), jnp.int32),
            pltpu.VMEM((2, T, W, C), BF16),
            pltpu.VMEM((2, T, W, C), BF16),
            pltpu.VMEM((MESSAGES, ROWS, C), BF16),
            pltpu.VMEM((MESSAGES, ROWS, C), BF16),
            pltpu.VMEM((ROWS, C), BF16),
            pltpu.VMEM((ROWS, C), BF16),
            dma((T,)),
            dma((T,)),
            dma,
            dma,
            dma((2,)),
            dma((T - 1, 2)),
            dma((T, 2)),
            dma((T, 2)),
            dma((T, 2)),
            dma((T - 1, 2)),
            dma((2,)),
            dma((2,)),
            dma((MESSAGES,)),
            dma((MESSAGES,)),
            dma,
            dma,
        ],
        compiler_params=pltpu.CompilerParams(
            collective_id=0, has_side_effects=True, vmem_limit_bytes=48 * 2**20
        ),
        cost_estimate=pl.CostEstimate(
            flops=4 * T * PX * 9 * C * C, bytes_accessed=6 * 2**20, transcendentals=0
        ),
    )(
        saved_inputs.reshape(T, PX, C),
        relu_mask.reshape(T, PX, C),
        grads_in.reshape(PX, C),
        head_grads.reshape(T - 1, PX, C),
        kernels.reshape(9 * C, C),
        bn_scale,
    )
    return kernel_grads[None], outgoing.reshape(1, H, W, C)


def solution(mesh):
    return jax.shard_map(
        per_device,
        mesh=mesh,
        in_specs=(
            P("section", None, "tile", None, None),
            P("section", None, "tile", None, None),
            P("section", "tile", None, None),
            P(None, "tile", None, None),
            P("section", None, None, None, None),
            P("section", None),
        ),
        out_specs=(P("section", "tile", None), P("section", "tile", None, None)),
        check_vma=False,
    )
```

time: 383 us -> 69.1 us (0.18)
  the two profiles are of different devices: /device:TPU:1 before, /device:TPU:64 now
where the time goes in v1:
time: 69.1 us; the launch traced here: 68.8 us
  Pallas kernels  60 us (87%)
  local copies, waits for them, and re-layouts  8.2 us (12%)
    pallas_call x1, Pallas kernels, per_device(): pl.pallas_call(kernel, out_shape=(jax.ShapeDtypeStruct((ROWS, C), F32), j...  60 us
    unnamed x14, local copies, waits for them, and re-layouts  8.2 us

profile of v1, /device:TPU:64, one launch (start us, length us, event | category | flops | bytes accessed | tf_op | source)
XLA Modules:
  0.0 68.8 jit_solution(2754775198514972252)
XLA Ops:
  0.6 0.0 copy-start
  0.6 1.6 %copy-done = s32[1,4,16,32,256]{4,3,2,1,0:T(8,128)S(1)} copy-done((s32[1,4,16,32,256]{4,3,2,1,0:T(8,128)S(1)}, s32[1,4,16,32,256]{4,3,2,1,0:T(8,128)}, u32[]{:S(2)}) %copy-start) | copy-done | bytes 2097176
  2.2 0.0 copy-start.1
  2.2 1.3 %copy-done.1 = bf16[1,3,3,256,256]{4,3,2,1,0:T(8,128)(2,1)S(1)} copy-done((bf16[1,3,3,256,256]{4,3,2,1,0:T(8,128)(2,1)S(1)}, bf16[1,3,3,256,256]{4,3,2,1,0:T(8,128)(2,1)}, u32[]{:S(2)}) %copy-start.1) | copy-done | bytes 1179672
  3.5 0.0 copy-start.2
  3.5 1.2 %copy-done.2 = bf16[1,4,16,32,256]{4,3,2,1,0:T(8,128)(2,1)S(1)} copy-done((bf16[1,4,16,32,256]{4,3,2,1,0:T(8,128)(2,1)S(1)}, bf16[1,4,16,32,256]{4,3,2,1,0:T(8,128)(2,1)}, u32[]{:S(2)}) %copy-start.2) | copy-done | bytes 1048600
  4.7 0.0 copy-start.3
  4.7 1.1 %copy-done.3 = bf16[3,16,32,256]{3,2,1,0:T(8,128)(2,1)S(1)} copy-done((bf16[3,16,32,256]{3,2,1,0:T(8,128)(2,1)S(1)}, bf16[3,16,32,256]{3,2,1,0:T(8,128)(2,1)}, u32[]{:S(2)}) %copy-start.3) | copy-done | bytes 786456
  5.9 0.0 copy-start.4
  5.9 0.9 %copy-done.4 = bf16[1,16,32,256]{3,2,1,0:T(8,128)(2,1)S(1)} copy-done((bf16[1,16,32,256]{3,2,1,0:T(8,128)(2,1)S(1)}, bf16[1,16,32,256]{3,2,1,0:T(8,128)(2,1)}, u32[]{:S(2)}) %copy-start.4) | copy-done | bytes 262168
  6.8 0.0 copy-start.5
  6.8 0.7 copy-done.5
  7.5 60.0 %shard_map.77 = (f32[144,256]{1,0:T(8,128)S(1)}, bf16[512,256]{1,0:T(8,128)(2,1)S(1)}) custom-call(bf16[4,512,256]{2,1,0:T(8,128)(2,1)S(1)} %bitcast.11, s32[4,512,256]{2,1,0:T(8,128)S(1)} %bitcast.9, bf16[512,256]{1,0:T(8,128)(2,1)S(1)} %bitcast.13, bf16[3,512,256]{2,1,0:T(8,128)(2,1)S(1)} %bitcast.12, bf16[2304,256]{1,0:T(8,128)(2,1)S(1)} %bitcast.10, ...), custom_call_target="tpu_custom_call" | custom-call | flops 4831838208 | bytes 6291456 | tf_op jit(solution)/shard_map/pallas_call | solution.py:366
  67.5 0.7 copy.10
  68.1 0.7 %copy.11 = bf16[1,16,32,256]{3,2,1,0:T(8,128)(2,1)} copy(bf16[1,16,32,256]{3,2,1,0:T(8,128)(2,1)S(1)} %bitcast.7) | data formatting | bytes 524288
Async XLA Ops:
  0.6 1.6 %copy-start = (s32[1,4,16,32,256]{4,3,2,1,0:T(8,128)S(1)}, s32[1,4,16,32,256]{4,3,2,1,0:T(8,128)}, u32[]{:S(2)}) copy-start(s32[1,4,16,32,256]{4,3,2,1,0:T(8,128)} %param.7) | copy-start | bytes 6291460
  2.2 1.3 %copy-start.1 = (bf16[1,3,3,256,256]{4,3,2,1,0:T(8,128)(2,1)S(1)}, bf16[1,3,3,256,256]{4,3,2,1,0:T(8,128)(2,1)}, u32[]{:S(2)}) copy-start(bf16[1,3,3,256,256]{4,3,2,1,0:T(8,128)(2,1)} %param.10) | copy-start | bytes 3538948
  3.5 1.2 %copy-start.2 = (bf16[1,4,16,32,256]{4,3,2,1,0:T(8,128)(2,1)S(1)}, bf16[1,4,16,32,256]{4,3,2,1,0:T(8,128)(2,1)}, u32[]{:S(2)}) copy-start(bf16[1,4,16,32,256]{4,3,2,1,0:T(8,128)(2,1)} %param.6) | copy-start | bytes 3145732
  4.7 1.1 %copy-start.3 = (bf16[3,16,32,256]{3,2,1,0:T(8,128)(2,1)S(1)}, bf16[3,16,32,256]{3,2,1,0:T(8,128)(2,1)}, u32[]{:S(2)}) copy-start(bf16[3,16,32,256]{3,2,1,0:T(8,128)(2,1)} %param.9) | copy-start | bytes 2359300
  5.9 0.9 %copy-start.4 = (bf16[1,16,32,256]{3,2,1,0:T(8,128)(2,1)S(1)}, bf16[1,16,32,256]{3,2,1,0:T(8,128)(2,1)}, u32[]{:S(2)}) copy-start(bf16[1,16,32,256]{3,2,1,0:T(8,128)(2,1)} %param.8) | copy-start | bytes 786436
  6.8 0.7 copy-start.5

commit v2 on v0

v2 whole, which is shorter than its diff:
```python
import functools
import math

import jax
import jax.numpy as jnp
from jax import lax
from jax.experimental import pallas as pl
from jax.experimental.pallas import tpu as pltpu
from jax.sharding import PartitionSpec as P

MESH = pl.DeviceIdType.MESH
F32 = jnp.float32
BF16 = jnp.bfloat16
T, H, W, C = 4, 16, 32, 256
PX = H * W
LEAD = 2
GRID = PX + 2 * LEAD * W
SECTIONS, TILES, RING = 32, 16, 8
ROWS = 9 * C // TILES
PIECES = ((0, 80), (80, 64))
PLAN = {
    "F4+": (1, 4, 1, None), "F3+": (1, 3, 1, "F4+"), "F2+": (1, 2, 1, "F3+"), "F1+": (1, 1, 1, "F2+"),
    "F3-": (1, 3, -1, None), "F2-": (1, 2, -1, "F3-"), "F1-": (1, 1, -1, "F2-"), "F0": (1, 0, 0, None),
    "N3+": (0, 3, 1, None), "N2+": (0, 2, 1, "N3+"), "N1+": (0, 1, 1, "N2+"),
    "N4-": (0, 4, -1, None), "N3-": (0, 3, -1, "N4-"), "N2-": (0, 2, -1, "N3-"), "N1-": (0, 1, -1, "N2-"),
}
ORDER = (
    "F4+", "F3-", "N4-", "N3+", "F0", "F3+", "F2-", "N3-", "N2+", "F2+", "F1-", "N2-", "F1+", "N1+", "N1-",
)
FIRST = 4
TN = (((0,), (0,)), ((), ()))
NT = (((1,), (1,)), ((), ()))


def loop(count, step, start=0):
    def one(i, carry):
        step(i)
        return carry

    lax.fori_loop(start, count, one, 0)


def kernel(
    x_hbm, m_hbm, gin_hbm, head_hbm, w_hbm, sc_hbm, kg_ref, out_ref,
    xv, mv, wv, sv, gb, pg, bg, acc, xt, edge_i, edge, mh, sbuf, rbuf,
    ld_x, ld_m, ld_w, ld_s, ld_e,
    gm_send, gm_recv, ge_send, ge_recv, gd_send, gd_recv, hh_send,
    p0_send, p0_recv, mh_send, mh_recv, rs_send, rs_recv,
):
    s = lax.axis_index("section")
    j = lax.axis_index("tile")
    z, y = j // RING, j % RING
    has_tile = (j > 0, j < TILES - 1)
    sends, takes = s > 0, s < SECTIONS - 1
    top = s == SECTIONS - 1
    last = T - 1

    def ring(distance, other=0):
        row = (z + other) % 2
        return row * RING + (y + distance + RING) % RING

    def beside(side):
        return j - 1 + 2 * side

    barrier = pltpu.get_barrier_semaphore()

    def greet(section, tile):
        pl.semaphore_signal(barrier, inc=1, device_id=(section, tile), device_id_type=MESH)

    for distance, other in ((1, 0), (-1, 0), (0, 1), (1, 1), (-1, 1)):
        greet(s, ring(distance, other))
    for side in range(2):
        pl.when(has_tile[side])(lambda side=side: greet(s, beside(side)))

    @pl.when(takes)
    def _():
        greet(s + 1, j)
        for side in range(2):
            pl.when(has_tile[side])(lambda side=side: greet(s + 1, beside(side)))

    def rows(i, count=1, lead=LEAD):
        return pl.ds((i + lead) * W, count * W)

    def local(src, dst, sem):
        return pltpu.make_async_copy(src, dst, sem)

    def to_tile(src, dst, send, recv, section, tile):
        return pltpu.make_async_remote_copy(
            src_ref=src, dst_ref=dst, send_sem=send, recv_sem=recv,
            device_id=(section, tile), device_id_type=MESH,
        )

    def edge_load(side):
        return local(
            m_hbm.at[pl.ds(1, T - 1), rows(side * (H - 2), 2, 0), :], edge_i.at[side], ld_e.at[side]
        )

    def first_load(h):
        return local(
            gin_hbm.at[rows(h * (H // 2), H // 2, 0)], gb.at[0, rows(h * (H // 2), H // 2)], gm_recv.at[0, h]
        )

    def mask_load(t):
        return local(m_hbm.at[t], mv.at[t], ld_m.at[t])

    def x_load(t):
        return local(x_hbm.at[t], xv.at[t], ld_x.at[t])

    w_load = local(w_hbm, wv, ld_w)
    s_load = local(sc_hbm, sv, ld_s)
    s_load.start()
    first_load(0).start()
    first_load(1).start()
    mask_load(0).start()
    edge_load(0).start()
    edge_load(1).start()
    w_load.start()
    x_load(0).start()
    for t in range(1, T):
        mask_load(t).start()
        x_load(t).start()

    inner = {0: ((1, 7), (8, 7)), 1: ((2, 5), (7, 7)), 2: ((1, 7), (8, 7))}
    ends = {0: (-1, H - 1), 1: (0, H - 2), 2: (-1, H - 1)}

    def pass_inner(t, h):
        first, count = inner[t][h]
        return to_tile(
            bg.at[t, rows(first, count, 1)], gb.at[t + 1, rows(first, count)],
            gm_send.at[t, h], gm_recv.at[t + 1, h], s - 1, j,
        )

    def pass_end(t, side):
        return to_tile(
            bg.at[t, rows(ends[t][side], 2, 1)], gb.at[t + 1, rows(ends[t][side], 2)],
            ge_send.at[t, side], ge_recv.at[t + 1, side], s - 1, j,
        )

    def far(t, side):
        return gb.at[t, rows(H - (H + 2) * side, 2)]

    def pass_aside(side):
        return to_tile(
            bg.at[1, rows(ends[1][side], 2, 1)], far(2, side),
            gd_send.at[side], gd_recv.at[1 - side], s - 1, beside(side),
        )

    def first_aside(side):
        return to_tile(
            pg.at[1, rows(side * (H - 2), 2)], far(0, side),
            p0_send.at[side], p0_recv.at[1 - side], s, beside(side),
        )

    def mask_aside(side):
        return to_tile(
            edge.at[side], mh.at[1 - side], mh_send.at[side], mh_recv.at[1 - side], s, beside(side)
        )

    def head_local(t, first, count, sem):
        return local(head_hbm.at[t, rows(first, count, 0)], gb.at[t + 1, rows(first, count)], sem)

    def head_aside(t, side):
        if t == 1:
            src, dst, recv = rows(side * (H - 2), 2, 0), far(2, side), gd_recv.at[1 - side]
        else:
            src, dst, recv = rows(side * (H - 1), 1, 0), gb.at[t + 1, rows(H - (H + 1) * side)], ge_recv.at[t + 1, 1 - side]
        return to_tile(head_hbm.at[t, src], dst, hh_send.at[t, side], recv, s, beside(side))

    @pl.when(top)
    def _():
        for t in range(T - 1):
            for h in range(2):
                head_local(t, *inner[t][h], gm_recv.at[t + 1, h]).start()
            for side in range(2):
                sem = ge_recv.at[t + 1, side]
                if t == 1:
                    head_local(t, ends[t][side], 2, sem).start()
                else:
                    head_local(t, side * (H - 1), 1, sem).start()

                    @pl.when(jnp.logical_not(has_tile[side]))
                    def _(t=t, side=side, sem=sem):
                        local(
                            head_hbm.at[t, rows(side * (H - 1), 1, 0)],
                            gb.at[t + 1, rows(side * (H + 1) - 1)], sem,
                        ).start()

    def put(t, row, value):
        count = value.shape[0]
        column = lax.broadcasted_iota(jnp.int32, (count, C), 0) % W
        dst = pl.ds((row + LEAD) * W, count)
        right = jnp.where(column == W - 1, 0.0, pltpu.roll(value, count - 1, 0))
        left = jnp.where(column == 0, 0.0, pltpu.roll(value, 1, 0))
        pg[3 * t, dst, :] = right.astype(BF16)
        pg[3 * t + 1, dst, :] = value.astype(BF16)
        pg[3 * t + 2, dst, :] = left.astype(BF16)

    s_load.wait()
    scales = sv[...]

    def own_rows(t, first, count):
        grads = gb[t, rows(first, count), :].astype(F32)
        put(t, first, jnp.where(mv[t, rows(first, count, 0), :] != 0, grads * scales, 0.0))

    depth = (2, 1, 2, 1)
    mask_at = (None, 0, 1, 3)

    def beyond(t, side):
        count = depth[t]
        first = H if side else -count

        @pl.when(has_tile[side])
        def _():
            grads = gb[t, rows(first, count), :].astype(F32)
            if t:
                grads = grads * mh[side, rows(mask_at[t], count, 0), :].astype(F32) * scales
            put(t, first, grads)

        @pl.when(jnp.logical_not(has_tile[side]))
        def _():
            for b in range(3):
                pg[3 * t + b, rows(first, count), :] = jnp.zeros((count * W, C), BF16)

    def conv(t, starts, count):
        total = None
        for a in range(3):
            for b in range(3):
                parts = [pg[3 * t + b, rows(i + 1 - a, count), :] for i in starts]
                term = lax.dot_general(
                    parts[0] if len(parts) == 1 else jnp.concatenate(parts, axis=0),
                    wv[(3 * a + b) * C : (3 * a + b + 1) * C, :],
                    NT, preferred_element_type=F32,
                )
                total = term if total is None else total + term
        return total.astype(BF16)

    def inner_part(t, h):
        first, count = inner[t][h]
        bg[t, rows(first, count, 1), :] = conv(t, [first], count)
        pl.when(sends)(lambda: pass_inner(t, h).start())

    def end_parts(t):
        both = conv(t, ends[t], 2)
        for side in range(2):
            bg[t, rows(ends[t][side], 2, 1), :] = both[side * 2 * W : (side + 1) * 2 * W]

        @pl.when(sends)
        def _():
            for side in range(2):
                if t == 1:
                    pl.when(has_tile[side])(lambda side=side: pass_aside(side).start())
            for side in range(2):
                pass_end(t, side).start()

    def kernel_term(t):
        def one(a):
            taps = pl.ds(pl.multiple_of((LEAD + 1 - a) * W, W), PX)
            for b in range(3):
                dst = pl.ds(pl.multiple_of((3 * a + b) * C, C), C)
                acc[dst, :] += lax.dot_general(
                    xv[t], pg[3 * t + b, taps, :], TN, preferred_element_type=F32
                )

        loop(3, one)

    def got_inner(t, h):
        first, count = inner[t - 1][h]
        local(head_hbm.at[0, rows(first, count, 0)], gb.at[t, rows(first, count)], gm_recv.at[t, h]).wait()

    def got_end(t, side):
        local(head_hbm.at[0, rows(0, 2, 0)], gb.at[t, rows(ends[t - 1][side], 2)], ge_recv.at[t, side]).wait()

    first_load(0).wait()
    first_load(1).wait()
    mask_load(0).wait()
    own_rows(0, 0, 8)
    own_rows(0, 8, 8)
    for side in range(2):
        edge_load(side).wait()
        pick = pl.ds(side * W, W)
        edge[side, 0:W, :] = edge_i[side, 0, pick, :].astype(BF16)
        edge[side, W : 3 * W, :] = edge_i[side, 1, :, :].astype(BF16)
        edge[side, 3 * W : 4 * W, :] = edge_i[side, 2, pick, :].astype(BF16)

    beside_count = has_tile[0].astype(jnp.int32) + has_tile[1].astype(jnp.int32)
    pl.semaphore_wait(barrier, 5 + beside_count + jnp.where(sends, beside_count + 1, 0))

    for side in range(2):
        pl.when(has_tile[side])(lambda side=side: first_aside(side).start())
    for side in range(2):

        @pl.when(has_tile[side])
        def _(side=side):
            mask_aside(side).start()

            @pl.when(top)
            def _():
                for t in range(T - 1):
                    head_aside(t, side).start()

    w_load.wait()
    inner_part(0, 0)
    inner_part(0, 1)

    def clear(i):
        acc[pl.ds(pl.multiple_of(i * C, C), C), :] = jnp.zeros((C, C), F32)

    loop(9, clear)
    for side in range(2):
        pl.when(has_tile[side])(
            lambda side=side: local(gin_hbm.at[rows(0, 2, 0)], far(0, 1 - side), p0_recv.at[side]).wait()
        )
        beyond(0, side)
    end_parts(0)
    x_load(0).wait()
    kernel_term(0)

    mask_load(1).wait()
    got_inner(1, 0)
    own_rows(1, 1, 7)
    inner_part(1, 0)
    got_inner(1, 1)
    own_rows(1, 8, 7)
    inner_part(1, 1)
    for side in range(2):
        pl.when(has_tile[side])(
            lambda side=side: local(edge.at[side], mh.at[side], mh_recv.at[side]).wait()
        )
        got_end(1, side)
        own_rows(1, side * (H - 1), 1)
        beyond(1, side)
    end_parts(1)
    x_load(1).wait()
    kernel_term(1)

    mask_load(2).wait()
    got_inner(2, 0)
    own_rows(2, 2, 5)
    got_inner(2, 1)
    own_rows(2, 7, 7)
    for side in range(2):
        got_end(2, side)
        own_rows(2, side * (H - 2), 2)
    inner_part(2, 0)
    inner_part(2, 1)
    for side in range(2):
        pl.when(has_tile[side])(
            lambda side=side: local(gin_hbm.at[rows(0, 2, 0)], far(2, 1 - side), gd_recv.at[side]).wait()
        )
        beyond(2, side)
    end_parts(2)
    x_load(2).wait()
    kernel_term(2)

    x_load(last).wait()
    turned = xv[last].T
    xt[0:C, :] = turned
    xt[C : 2 * C, :] = turned
    mask_load(last).wait()
    got_inner(last, 0)
    own_rows(last, 1, 7)
    got_inner(last, 1)
    own_rows(last, 8, 7)
    for side in range(2):
        got_end(last, side)
        own_rows(last, side * (H - 1), 1)
        beyond(last, side)

    def block_row(name):
        kind, away, way, _ = PLAN[name]
        return ring(way * away, kind) * ROWS

    def piece(name, part, whole=False):
        start, count = (0, ROWS) if whole else PIECES[part]
        return pl.ds(pl.multiple_of(block_row(name) + start, 16), count)

    def message(name, part):
        kind, away, way, _ = PLAN[name]
        i = ORDER.index(name)
        at = pl.ds(*PIECES[part])
        crosses = kind == 1 and away <= 1
        return to_tile(
            sbuf.at[i, at], rbuf.at[i, at], rs_send.at[i, part], rs_recv.at[i, part],
            s, ring(way, 1 if crosses else 0),
        )

    def first_message(name):
        row0 = block_row(name)
        tap = row0 // C
        at = pl.multiple_of(row0 - tap * C, 16)
        lhs = xt[pl.ds(at, ROWS), :]

        def term(tap):
            a, b = tap // 3, tap % 3
            taps = pl.ds(pl.multiple_of((LEAD + 1 - a) * W, W), PX)
            return jnp.dot(lhs, pg[3 * last + b, taps, :], preferred_element_type=F32)

        row = lax.broadcasted_iota(jnp.int32, (ROWS, C), 0) + at
        own = jnp.where(row < C, term(tap), term(jnp.minimum(tap + 1, 8)))
        sbuf[ORDER.index(name)] = (acc[piece(name, 0, True), :] + own).astype(BF16)
        for part in range(2):
            message(name, part).start()

    def later_message(name, part):
        total = acc[piece(name, part), :]
        before = PLAN[name][3]
        at = pl.ds(*PIECES[part])
        if before:
            message(before, part).wait_recv()
            total = total + rbuf[ORDER.index(before), at, :].astype(F32)
        sbuf[ORDER.index(name), at, :] = total.astype(BF16)
        message(name, part).start()

    for name in ORDER[:FIRST]:
        first_message(name)
    kernel_term(last)
    for name in ORDER[FIRST:]:
        for part in range(2):
            later_message(name, part)
        if name == "F1-":
            out_ref[...] = conv(last, [0], H)

    for part in range(2):
        start, count = PIECES[part]
        at = pl.ds(start, count)
        total = acc[pl.ds(pl.multiple_of(j * ROWS + start, 16), count), :]
        for name in ("F0", "F1-", "N1+", "F1+", "N1-"):
            message(name, part).wait_recv()
            total = total + rbuf[ORDER.index(name), at, :].astype(F32)
        kg_ref[at, :] = total * (1.0 / math.sqrt(T * TILES * PX))

    for name in ORDER:
        for part in range(2):
            message(name, part).wait_send()
    for side in range(2):

        @pl.when(has_tile[side])
        def _(side=side):
            first_aside(side).wait_send()
            mask_aside(side).wait_send()
            pl.when(sends)(lambda: pass_aside(side).wait_send())

            @pl.when(top)
            def _():
                for t in range(T - 1):
                    head_aside(t, side).wait_send()

    @pl.when(sends)
    def _():
        for t in range(T - 1):
            for k in range(2):
                pass_inner(t, k).wait_send()
                pass_end(t, k).wait_send()


def per_device(saved_inputs, relu_mask, grads_in, head_grads, kernels, bn_scale):
    any_space = pl.BlockSpec(memory_space=pl.ANY)
    vmem = pl.BlockSpec(memory_space=pltpu.VMEM)
    dma = pltpu.SemaphoreType.DMA
    kernel_grads, outgoing = pl.pallas_call(
        kernel,
        out_shape=(
            pltpu.VMEM((ROWS, C), F32),
            pltpu.VMEM((PX, C), BF16),
        ),
        in_specs=[any_space] * 6,
        out_specs=(vmem, vmem),
        scratch_shapes=[
            pltpu.VMEM((T, PX, C), BF16),
            pltpu.VMEM((T, PX, C), jnp.int32),
            pltpu.VMEM((9 * C, C), BF16),
            pltpu.VMEM((1, C), F32),
            pltpu.VMEM((T, GRID, C), BF16),
            pltpu.VMEM((3 * T, GRID, C), BF16),
            pltpu.VMEM((T - 1, PX + 2 * W, C), BF16),
            pltpu.VMEM((9 * C, C), F32),
            pltpu.VMEM((2 * C, PX), BF16),
            pltpu.VMEM((2, T - 1, 2 * W, C), jnp.int32),
            pltpu.VMEM((2, 4 * W, C), BF16),
            pltpu.VMEM((2, 4 * W, C), BF16),
            pltpu.VMEM((len(ORDER), ROWS, C), BF16),
            pltpu.VMEM((len(ORDER), ROWS, C), BF16),
            dma((T,)),
            dma((T,)),
            dma,
            dma,
            dma((2,)),
            dma((T - 1, 2)),
            dma((T, 2)),
            dma((T - 1, 2)),
            dma((T, 2)),
            dma((2,)),
            dma((2,)),
            dma((T - 1, 2)),
            dma((2,)),
            dma((2,)),
            dma((2,)),
            dma((2,)),
            dma((len(ORDER), 2)),
            dma((len(ORDER), 2)),
        ],
        compiler_params=pltpu.CompilerParams(
            collective_id=0, has_side_effects=True, vmem_limit_bytes=62 * 2**20
        ),
        cost_estimate=pl.CostEstimate(
            flops=4 * T * PX * 9 * C * C, bytes_accessed=6 * 2**20, transcendentals=0
        ),
    )(
        saved_inputs.reshape(T, PX, C),
        relu_mask.reshape(T, PX, C),
        grads_in.reshape(PX, C),
        head_grads.reshape(T - 1, PX, C),
        kernels.reshape(9 * C, C),
        bn_scale,
    )
    return kernel_grads[None], outgoing.reshape(1, H, W, C)


def solution(mesh):
    return jax.shard_map(
        per_device,
        mesh=mesh,
        in_specs=(
            P("section", None, "tile", None, None),
            P("section", None, "tile", None, None),
            P("section", "tile", None, None),
            P(None, "tile", None, None),
            P("section", None, None, None, None),
            P("section", None),
        ),
        out_specs=(P("section", "tile", None), P("section", "tile", None, None)),
        check_vma=False,
    )
```

time: 383 us -> 52.6 us (0.14); the launches traced: 377 us -> 52.4 us
  waiting for transfers between devices: 268 us -> 0 us
  starting transfers between devices: 64.4 us -> 0 us
  Pallas kernels: 0 us -> 50.4 us
  between operations: 15.1 us -> 0.64 us
  local copies, waits for them, and re-layouts: 12.8 us -> 1.37 us
  other arithmetic: 9.45 us -> 0 us
  matrix products: 7.68 us -> 0 us
    reduce_scatter x1 -> x0, waiting for transfers between devices: 234 us -> none  [sum_kernels(): lax.psum_scatter(lax.dot_general(all_patches, all_grads, (((0,), (0,)), (...]
    ppermute x19 -> x0, starting transfers between devices: 64.4 us -> none  [the longest x8 41.5 us: with_halo(): before = lax.ppermute(last, axis, up)]
    pallas_call x0 -> x1, Pallas kernels: none -> 50.4 us  [per_device(): pl.pallas_call(kernel, out_shape=(pltpu.VMEM((ROWS, C), F32), pltpu.VMEM(...]
    ppermute x19 -> x0, waiting for transfers between devices: 34.2 us -> none  [the longest x8 22.1 us: with_halo(): after = lax.ppermute(leading, axis, down)]
    dot_general x5 -> x0, matrix products: 7.68 us -> none  [the longest x1 3.86 us: sum_kernels(): lax.dot_general(all_patches, all_grads, (((0,), (0,)), ((), ())), preferr...]
    slice x10 -> x0, local copies, waits for them, and re-layouts: 5.63 us -> none  [the longest x1 2.57 us: per_device(): framed = with_halo(inputs[tick], (('tile', 0),), 1)]
    unnamed x93 -> x2, local copies, waits for them, and re-layouts: 5.56 us -> 1.37 us
  transfers between devices with their start and end apart: 20 -> 0, of which waited for: 6 -> 0; matrix products, arithmetic and copies ran while one was open for 5% -> 0% of each run, Pallas kernels for 0% -> 0%
where the time goes in v2:
time: 52.6 us; the launch traced here: 52.4 us
  Pallas kernels  50.4 us (96%)
  local copies, waits for them, and re-layouts  1.37 us (3%)
  between operations  0.64 us (1%)
    pallas_call x1, Pallas kernels, per_device(): pl.pallas_call(kernel, out_shape=(pltpu.VMEM((ROWS, C), F32), pltpu.VMEM(...  50.4 us
    unnamed x2, local copies, waits for them, and re-layouts  1.37 us

profile of v2, /device:TPU:1, one launch (start us, length us, event | category | flops | bytes accessed | tf_op | source)
XLA Modules:
  0.0 52.4 jit_solution(6527012456206806899)
XLA Ops:
  0.6 50.4 %shard_map.77 = (f32[144,256]{1,0:T(8,128)S(1)}, bf16[512,256]{1,0:T(8,128)(2,1)S(1)}) custom-call(bf16[4,512,256]{2,1,0:T(8,128)(2,1)} %bitcast.11, s32[4,512,256]{2,1,0:T(8,128)} %bitcast.9, bf16[512,256]{1,0:T(8,128)(2,1)} %bitcast.13, bf16[3,512,256]{2,1,0:T(8,128)(2,1)} %bitcast.12, bf16[2304,256]{1,0:T(8,128)(2,1)} %bitcast.10, f32[1,256]{1,0:T(1,128)} %sc_hbm.1), custom_call_target="tpu_custom_call" | custom-call | flops 4831838208 | bytes 6291456 | tf_op jit(solution)/shard_map/pallas_call | solution.py:460
  51.1 0.7 %copy.10 = f32[1,144,256]{2,1,0:T(8,128)} copy(f32[1,144,256]{2,1,0:T(8,128)S(1)} %bitcast.8) | data formatting | bytes 294912
  51.7 0.7 %copy.11 = bf16[1,16,32,256]{3,2,1,0:T(8,128)(2,1)} copy(bf16[1,16,32,256]{3,2,1,0:T(8,128)(2,1)S(1)} %bitcast.7) | data formatting | bytes 524288

commit v3 on v2

--- a/solution.py
+++ b/solution.py
@@ -13,7 +13,7 @@
 BF16 = jnp.bfloat16
 T, H, W, C = 4, 16, 32, 256
 PX = H * W
-LEAD = 2
+LEAD = 4
 GRID = PX + 2 * LEAD * W
 SECTIONS, TILES, RING = 32, 16, 8
 ROWS = 9 * C // TILES
@@ -42,15 +42,17 @@
 
 def kernel(
     x_hbm, m_hbm, gin_hbm, head_hbm, w_hbm, sc_hbm, kg_ref, out_ref,
-    xv, mv, wv, sv, gb, pg, bg, acc, xt, edge_i, edge, mh, sbuf, rbuf,
-    ld_x, ld_m, ld_w, ld_s, ld_e,
-    gm_send, gm_recv, ge_send, ge_recv, gd_send, gd_recv, hh_send,
+    xv, mv, wv, sv, gb, pg, bg, acc, xt, edge, mh, sbuf, rbuf,
+    ld_x, ld_m, ld_w, ld_s,
+    gm_send, gm_recv, ge_send, ge_recv, gd_send, gd_recv, gx_send, gx_recv, hh_send, hx_send,
     p0_send, p0_recv, mh_send, mh_recv, rs_send, rs_recv,
 ):
     s = lax.axis_index("section")
     j = lax.axis_index("tile")
     z, y = j // RING, j % RING
     has_tile = (j > 0, j < TILES - 1)
+    seam = (j == RING, j == RING - 1)
+    near = tuple(jnp.logical_and(a, jnp.logical_not(b)) for a, b in zip(has_tile, seam))
     sends, takes = s > 0, s < SECTIONS - 1
     top = s == SECTIONS - 1
     last = T - 1
@@ -67,16 +69,16 @@
     def greet(section, tile):
         pl.semaphore_signal(barrier, inc=1, device_id=(section, tile), device_id_type=MESH)
 
+    for side in range(2):
+        pl.when(has_tile[side])(lambda side=side: greet(s, beside(side)))
     for distance, other in ((1, 0), (-1, 0), (0, 1), (1, 1), (-1, 1)):
         greet(s, ring(distance, other))
-    for side in range(2):
-        pl.when(has_tile[side])(lambda side=side: greet(s, beside(side)))
 
     @pl.when(takes)
     def _():
         greet(s + 1, j)
         for side in range(2):
-            pl.when(has_tile[side])(lambda side=side: greet(s + 1, beside(side)))
+            pl.when(near[side])(lambda side=side: greet(s + 1, beside(side)))
 
     def rows(i, count=1, lead=LEAD):
         return pl.ds((i + lead) * W, count * W)
@@ -88,11 +90,6 @@
         return pltpu.make_async_remote_copy(
             src_ref=src, dst_ref=dst, send_sem=send, recv_sem=recv,
             device_id=(section, tile), device_id_type=MESH,
-        )
-
-    def edge_load(side):
-        return local(
-            m_hbm.at[pl.ds(1, T - 1), rows(side * (H - 2), 2, 0), :], edge_i.at[side], ld_e.at[side]
         )
 
     def first_load(h):
@@ -111,13 +108,10 @@
     s_load.start()
     first_load(0).start()
     first_load(1).start()
-    mask_load(0).start()
-    edge_load(0).start()
-    edge_load(1).start()
+    for t in range(T):
+        mask_load(t).start()
     w_load.start()
-    x_load(0).start()
-    for t in range(1, T):
-        mask_load(t).start()
+    for t in range(T):
         x_load(t).start()
 
     inner = {0: ((1, 7), (8, 7)), 1: ((2, 5), (7, 7)), 2: ((1, 7), (8, 7))}
@@ -126,28 +120,37 @@
     def pass_inner(t, h):
         first, count = inner[t][h]
         return to_tile(
-            bg.at[t, rows(first, count, 1)], gb.at[t + 1, rows(first, count)],
+            bg.at[t, rows(first, count, 3)], gb.at[t + 1, rows(first, count)],
             gm_send.at[t, h], gm_recv.at[t + 1, h], s - 1, j,
         )
 
     def pass_end(t, side):
         return to_tile(
-            bg.at[t, rows(ends[t][side], 2, 1)], gb.at[t + 1, rows(ends[t][side], 2)],
+            bg.at[t, rows(ends[t][side], 2, 3)], gb.at[t + 1, rows(ends[t][side], 2)],
             ge_send.at[t, side], ge_recv.at[t + 1, side], s - 1, j,
         )
 
-    def far(t, side):
-        return gb.at[t, rows(H - (H + 2) * side, 2)]
+    extra = ((-3, H + 1), (-2, H))
+
+    def pass_extra(t, side):
+        send, recv = ((gx_send, gx_recv), (gd_send, gd_recv))[t]
+        return to_tile(
+            bg.at[t, rows(extra[t][side], 2, 3)], gb.at[t + 1, rows(extra[t][side], 2)],
+            send.at[side], recv.at[side], s - 1, j,
+        )
+
+    def far(t, side, count=2):
+        return gb.at[t, rows(H - (H + count) * side, count)]
 
     def pass_aside(side):
         return to_tile(
-            bg.at[1, rows(ends[1][side], 2, 1)], far(2, side),
+            bg.at[1, rows(ends[1][side], 2, 3)], far(2, side),
             gd_send.at[side], gd_recv.at[1 - side], s - 1, beside(side),
         )
 
-    def first_aside(side):
-        return to_tile(
-            pg.at[1, rows(side * (H - 2), 2)], far(0, side),
+    def first_aside(side, count):
+        return to_tile(
+            pg.at[1, rows(side * (H - count), count)], far(0, side, count),
             p0_send.at[side], p0_recv.at[1 - side], s, beside(side),
         )
 
@@ -165,6 +168,12 @@
         else:
             src, dst, recv = rows(side * (H - 1), 1, 0), gb.at[t + 1, rows(H - (H + 1) * side)], ge_recv.at[t + 1, 1 - side]
         return to_tile(head_hbm.at[t, src], dst, hh_send.at[t, side], recv, s, beside(side))
+
+    def head_extra(side):
+        return to_tile(
+            head_hbm.at[0, rows(1 + side * (H - 4), 2, 0)], gb.at[1, rows(H + 1 - (H + 4) * side, 2)],
+            hx_send.at[side], gx_recv.at[1 - side], s, beside(side),
+        )
 
     @pl.when(top)
     def _():
@@ -202,24 +211,28 @@
         grads = gb[t, rows(first, count), :].astype(F32)
         put(t, first, jnp.where(mv[t, rows(first, count, 0), :] != 0, grads * scales, 0.0))
 
-    depth = (2, 1, 2, 1)
-    mask_at = (None, 0, 1, 3)
+    depth, seam_depth = (2, 1, 2, 1), (4, 3, 2, 1)
+    mask_at = (None, 0, 3, 5)
 
     def beyond(t, side):
-        count = depth[t]
-        first = H if side else -count
-
-        @pl.when(has_tile[side])
-        def _():
+        def fill(count):
+            first = H if side else -count
             grads = gb[t, rows(first, count), :].astype(F32)
             if t:
-                grads = grads * mh[side, rows(mask_at[t], count, 0), :].astype(F32) * scales
+                at = mask_at[t] + (0 if side else seam_depth[t] - count)
+                grads = grads * mh[side, rows(at, count, 0), :].astype(F32) * scales
             put(t, first, grads)
+
+        if t < 2:
+            pl.when(near[side])(lambda: fill(depth[t]))
+            pl.when(seam[side])(lambda: fill(seam_depth[t]))
+        else:
+            pl.when(has_tile[side])(lambda: fill(depth[t]))
 
         @pl.when(jnp.logical_not(has_tile[side]))
         def _():
             for b in range(3):
-                pg[3 * t + b, rows(first, count), :] = jnp.zeros((count * W, C), BF16)
+                pg[3 * t + b, rows(H if side else -depth[t], depth[t]), :] = jnp.zeros((depth[t] * W, C), BF16)
 
     def conv(t, starts, count):
         total = None
@@ -236,21 +249,28 @@
 
     def inner_part(t, h):
         first, count = inner[t][h]
-        bg[t, rows(first, count, 1), :] = conv(t, [first], count)
+        bg[t, rows(first, count, 3), :] = conv(t, [first], count)
         pl.when(sends)(lambda: pass_inner(t, h).start())
 
     def end_parts(t):
         both = conv(t, ends[t], 2)
         for side in range(2):
-            bg[t, rows(ends[t][side], 2, 1), :] = both[side * 2 * W : (side + 1) * 2 * W]
+            bg[t, rows(ends[t][side], 2, 3), :] = both[side * 2 * W : (side + 1) * 2 * W]
 
         @pl.when(sends)
         def _():
             for side in range(2):
                 if t == 1:
-                    pl.when(has_tile[side])(lambda side=side: pass_aside(side).start())
+                    pl.when(near[side])(lambda side=side: pass_aside(side).start())
             for side in range(2):
                 pass_end(t, side).start()
+            if t < 2:
+                for side in range(2):
+
+                    @pl.when(seam[side])
+                    def _(side=side):
+                        bg[t, rows(extra[t][side], 2, 3), :] = conv(t, [extra[t][side]], 2)
+                        pass_extra(t, side).start()
 
     def kernel_term(t):
         def one(a):
@@ -275,18 +295,20 @@
     mask_load(0).wait()
     own_rows(0, 0, 8)
     own_rows(0, 8, 8)
-    for side in range(2):
-        edge_load(side).wait()
-        pick = pl.ds(side * W, W)
-        edge[side, 0:W, :] = edge_i[side, 0, pick, :].astype(BF16)
-        edge[side, W : 3 * W, :] = edge_i[side, 1, :, :].astype(BF16)
-        edge[side, 3 * W : 4 * W, :] = edge_i[side, 2, pick, :].astype(BF16)
-
-    beside_count = has_tile[0].astype(jnp.int32) + has_tile[1].astype(jnp.int32)
-    pl.semaphore_wait(barrier, 5 + beside_count + jnp.where(sends, beside_count + 1, 0))
-
-    for side in range(2):
-        pl.when(has_tile[side])(lambda side=side: first_aside(side).start())
+    for t in range(1, T):
+        mask_load(t).wait()
+        count = seam_depth[t]
+        for side in range(2):
+            edge[side, rows(mask_at[t], count, 0), :] = mv[t, rows(side * (H - count), count, 0), :].astype(BF16)
+
+    def flags(pair):
+        return pair[0].astype(jnp.int32) + pair[1].astype(jnp.int32)
+
+    pl.semaphore_wait(barrier, 5 + flags(has_tile) + jnp.where(sends, flags(near) + 1, 0))
+
+    for side in range(2):
+        pl.when(near[side])(lambda side=side: first_aside(side, 2).start())
+        pl.when(seam[side])(lambda side=side: first_aside(side, 4).start())
     for side in range(2):
 
         @pl.when(has_tile[side])
@@ -297,6 +319,7 @@
             def _():
                 for t in range(T - 1):
                     head_aside(t, side).start()
+                pl.when(seam[side])(lambda: head_extra(side).start())
 
     w_load.wait()
     inner_part(0, 0)
@@ -306,25 +329,33 @@
         acc[pl.ds(pl.multiple_of(i * C, C), C), :] = jnp.zeros((C, C), F32)
 
     loop(9, clear)
-    for side in range(2):
-        pl.when(has_tile[side])(
-            lambda side=side: local(gin_hbm.at[rows(0, 2, 0)], far(0, 1 - side), p0_recv.at[side]).wait()
-        )
+
+    def got_far(t, side, count, sem):
+        local(gin_hbm.at[rows(0, count, 0)], far(t, 1 - side, count), sem.at[side]).wait()
+
+    for side in range(2):
+        pl.when(near[side])(lambda side=side: got_far(0, side, 2, p0_recv))
+        pl.when(seam[side])(lambda side=side: got_far(0, side, 4, p0_recv))
         beyond(0, side)
     end_parts(0)
-    x_load(0).wait()
-    kernel_term(0)
-
-    mask_load(1).wait()
+
     got_inner(1, 0)
     own_rows(1, 1, 7)
     inner_part(1, 0)
     got_inner(1, 1)
     own_rows(1, 8, 7)
     inner_part(1, 1)
+    x_load(0).wait()
+    kernel_term(0)
+
     for side in range(2):
         pl.when(has_tile[side])(
             lambda side=side: local(edge.at[side], mh.at[side], mh_recv.at[side]).wait()
+        )
+        pl.when(seam[side])(
+            lambda side=side: local(
+                gin_hbm.at[rows(0, 2, 0)], gb.at[1, rows(extra[0][side], 2)], gx_recv.at[side]
+            ).wait()
         )
         got_end(1, side)
         own_rows(1, side * (H - 1), 1)
@@ -333,7 +364,6 @@
     x_load(1).wait()
     kernel_term(1)
 
-    mask_load(2).wait()
     got_inner(2, 0)
     own_rows(2, 2, 5)
     got_inner(2, 1)
@@ -344,9 +374,7 @@
     inner_part(2, 0)
     inner_part(2, 1)
     for side in range(2):
-        pl.when(has_tile[side])(
-            lambda side=side: local(gin_hbm.at[rows(0, 2, 0)], far(2, 1 - side), gd_recv.at[side]).wait()
-        )
+        pl.when(has_tile[side])(lambda side=side: got_far(2, side, 2, gd_recv))
         beyond(2, side)
     end_parts(2)
     x_load(2).wait()
@@ -356,7 +384,6 @@
     turned = xv[last].T
     xt[0:C, :] = turned
     xt[C : 2 * C, :] = turned
-    mask_load(last).wait()
     got_inner(last, 0)
     own_rows(last, 1, 7)
     got_inner(last, 1)
@@ -436,14 +463,27 @@
 
         @pl.when(has_tile[side])
         def _(side=side):
-            first_aside(side).wait_send()
             mask_aside(side).wait_send()
-            pl.when(sends)(lambda: pass_aside(side).wait_send())
 
             @pl.when(top)
             def _():
                 for t in range(T - 1):
                     head_aside(t, side).wait_send()
+                pl.when(seam[side])(lambda: head_extra(side).wait_send())
+
+        @pl.when(near[side])
+        def _(side=side):
+            first_aside(side, 2).wait_send()
+            pl.when(sends)(lambda: pass_aside(side).wait_send())
+
+        @pl.when(seam[side])
+        def _(side=side):
+            first_aside(side, 4).wait_send()
+
+            @pl.when(sends)
+            def _():
+                pass_extra(0, side).wait_send()
+                pass_extra(1, side).wait_send()
 
     @pl.when(sends)
     def _():
@@ -472,26 +512,27 @@
             pltpu.VMEM((1, C), F32),
             pltpu.VMEM((T, GRID, C), BF16),
             pltpu.VMEM((3 * T, GRID, C), BF16),
-            pltpu.VMEM((T - 1, PX + 2 * W, C), BF16),
+            pltpu.VMEM((T - 1, PX + 6 * W, C), BF16),
             pltpu.VMEM((9 * C, C), F32),
             pltpu.VMEM((2 * C, PX), BF16),
-            pltpu.VMEM((2, T - 1, 2 * W, C), jnp.int32),
-            pltpu.VMEM((2, 4 * W, C), BF16),
-            pltpu.VMEM((2, 4 * W, C), BF16),
+            pltpu.VMEM((2, 6 * W, C), BF16),
+            pltpu.VMEM((2, 6 * W, C), BF16),
             pltpu.VMEM((len(ORDER), ROWS, C), BF16),
             pltpu.VMEM((len(ORDER), ROWS, C), BF16),
             dma((T,)),
             dma((T,)),
             dma,
             dma,
-            dma((2,)),
             dma((T - 1, 2)),
             dma((T, 2)),
             dma((T - 1, 2)),
             dma((T, 2)),
             dma((2,)),
             dma((2,)),
+            dma((2,)),
+            dma((2,)),
             dma((T - 1, 2)),
+            dma((2,)),
             dma((2,)),
             dma((2,)),
             dma((2,)),

time: 52.6 us -> 54.3 us (1.032)
  Pallas kernels: 50.4 us -> 52.1 us
    pallas_call x1, Pallas kernels: 50.4 us -> 52.1 us  [per_device(): pl.pallas_call(kernel, out_shape=(pltpu.VMEM((ROWS, C), F32), pltpu.VMEM(...]
where the time goes in v3:
time: 54.3 us; the launch traced here: 54.1 us
  Pallas kernels  52.1 us (96%)
  local copies, waits for them, and re-layouts  1.37 us (3%)
  between operations  0.64 us (1%)
    pallas_call x1, Pallas kernels, per_device(): pl.pallas_call(kernel, out_shape=(pltpu.VMEM((ROWS, C), F32), pltpu.VMEM(...  52.1 us
    unnamed x2, local copies, waits for them, and re-layouts  1.37 us

profile of v3, /device:TPU:1, one launch (start us, length us, event | category | flops | bytes accessed | tf_op | source)
XLA Modules:
  0.0 54.1 jit_solution(836696731173378332)
XLA Ops:
  0.6 52.1 %shard_map.77 = (f32[144,256]{1,0:T(8,128)S(1)}, bf16[512,256]{1,0:T(8,128)(2,1)S(1)}) custom-call(bf16[4,512,256]{2,1,0:T(8,128)(2,1)} %bitcast.11, s32[4,512,256]{2,1,0:T(8,128)} %bitcast.9, bf16[512,256]{1,0:T(8,128)(2,1)} %bitcast.13, bf16[3,512,256]{2,1,0:T(8,128)(2,1)} %bitcast.12, bf16[2304,256]{1,0:T(8,128)(2,1)} %bitcast.10, f32[1,256]{1,0:T(1,128)} %sc_hbm.1), custom_call_target="tpu_custom_call" | custom-call | flops 4831838208 | bytes 6291456 | tf_op jit(solution)/shard_map/pallas_call | solution.py:500
  52.8 0.7 %copy.10 = f32[1,144,256]{2,1,0:T(8,128)} copy(f32[1,144,256]{2,1,0:T(8,128)S(1)} %bitcast.8) | data formatting | bytes 294912
  53.4 0.7 %copy.11 = bf16[1,16,32,256]{3,2,1,0:T(8,128)(2,1)} copy(bf16[1,16,32,256]{3,2,1,0:T(8,128)(2,1)S(1)} %bitcast.7) | data formatting | bytes 524288

commit v4 on v2

--- a/solution.py
+++ b/solution.py
@@ -25,7 +25,7 @@
     "N4-": (0, 4, -1, None), "N3-": (0, 3, -1, "N4-"), "N2-": (0, 2, -1, "N3-"), "N1-": (0, 1, -1, "N2-"),
 }
 ORDER = (
-    "F4+", "F3-", "N4-", "N3+", "F0", "F3+", "F2-", "N3-", "N2+", "F2+", "F1-", "N2-", "F1+", "N1+", "N1-",
+    "F4+", "F3-", "N4-", "N3+", "F3+", "F2-", "N3-", "F0", "F2+", "F1-", "N2+", "N2-", "F1+", "N1+", "N1-",
 )
 FIRST = 4
 TN = (((0,), (0,)), ((), ()))
@@ -45,7 +45,7 @@
     xv, mv, wv, sv, gb, pg, bg, acc, xt, edge_i, edge, mh, sbuf, rbuf,
     ld_x, ld_m, ld_w, ld_s, ld_e,
     gm_send, gm_recv, ge_send, ge_recv, gd_send, gd_recv, hh_send,
-    p0_send, p0_recv, mh_send, mh_recv, rs_send, rs_recv,
+    p0_send, p0_recv, mh_send, mh_recv, rs_send, rs_recv, ready,
 ):
     s = lax.axis_index("section")
     j = lax.axis_index("tile")
@@ -67,10 +67,15 @@
     def greet(section, tile):
         pl.semaphore_signal(barrier, inc=1, device_id=(section, tile), device_id_type=MESH)
 
-    for distance, other in ((1, 0), (-1, 0), (0, 1), (1, 1), (-1, 1)):
-        greet(s, ring(distance, other))
     for side in range(2):
         pl.when(has_tile[side])(lambda side=side: greet(s, beside(side)))
+    greet(s, ring(1))
+    greet(s, ring(-1))
+
+    @pl.when(z == 0)
+    def _():
+        for distance in (-1, 0, 1):
+            greet(s, ring(distance, 1))
 
     @pl.when(takes)
     def _():
@@ -283,10 +288,22 @@
         edge[side, 3 * W : 4 * W, :] = edge_i[side, 2, pick, :].astype(BF16)
 
     beside_count = has_tile[0].astype(jnp.int32) + has_tile[1].astype(jnp.int32)
-    pl.semaphore_wait(barrier, 5 + beside_count + jnp.where(sends, beside_count + 1, 0))
+    pl.semaphore_wait(barrier, 2 + 3 * z + beside_count + jnp.where(sends, beside_count + 1, 0))
 
     for side in range(2):
         pl.when(has_tile[side])(lambda side=side: first_aside(side).start())
+
+    w_load.wait()
+    inner_part(0, 0)
+    inner_part(0, 1)
+
+    @pl.when(z == 1)
+    def _():
+        for distance in (-1, 0, 1):
+            pl.semaphore_signal(
+                ready, inc=1, device_id=(s, ring(distance, 1)), device_id_type=MESH
+            )
+
     for side in range(2):
 
         @pl.when(has_tile[side])
@@ -298,9 +315,6 @@
                 for t in range(T - 1):
                     head_aside(t, side).start()
 
-    w_load.wait()
-    inner_part(0, 0)
-    inner_part(0, 1)
 
     def clear(i):
         acc[pl.ds(pl.multiple_of(i * C, C), C), :] = jnp.zeros((C, C), F32)
@@ -312,8 +326,6 @@
         )
         beyond(0, side)
     end_parts(0)
-    x_load(0).wait()
-    kernel_term(0)
 
     mask_load(1).wait()
     got_inner(1, 0)
@@ -322,6 +334,8 @@
     got_inner(1, 1)
     own_rows(1, 8, 7)
     inner_part(1, 1)
+    x_load(0).wait()
+    kernel_term(0)
     for side in range(2):
         pl.when(has_tile[side])(
             lambda side=side: local(edge.at[side], mh.at[side], mh_recv.at[side]).wait()
@@ -415,9 +429,11 @@
         first_message(name)
     kernel_term(last)
     for name in ORDER[FIRST:]:
+        if name == "F0":
+            pl.when(z == 0)(lambda: pl.semaphore_wait(ready, 3))
         for part in range(2):
             later_message(name, part)
-        if name == "F1-":
+        if name == "F1+":
             out_ref[...] = conv(last, [0], H)
 
     for part in range(2):
@@ -451,6 +467,17 @@
             for k in range(2):
                 pass_inner(t, k).wait_send()
                 pass_end(t, k).wait_send()
+
+
+def store(kg_in, out_in, kg_hbm, out_hbm, kg_sem, out_sem):
+    copies = (
+        pltpu.make_async_copy(kg_in, kg_hbm, kg_sem),
+        pltpu.make_async_copy(out_in, out_hbm, out_sem),
+    )
+    for copy in copies:
+        copy.start()
+    for copy in copies:
+        copy.wait()
 
 
 def per_device(saved_inputs, relu_mask, grads_in, head_grads, kernels, bn_scale):
@@ -498,6 +525,7 @@
             dma((2,)),
             dma((len(ORDER), 2)),
             dma((len(ORDER), 2)),
+            pltpu.SemaphoreType.REGULAR,
         ],
         compiler_params=pltpu.CompilerParams(
             collective_id=0, has_side_effects=True, vmem_limit_bytes=62 * 2**20
@@ -513,6 +541,17 @@
         kernels.reshape(9 * C, C),
         bn_scale,
     )
+    kernel_grads, outgoing = pl.pallas_call(
+        store,
+        out_shape=(
+            jax.ShapeDtypeStruct((ROWS, C), F32),
+            jax.ShapeDtypeStruct((PX, C), BF16),
+        ),
+        in_specs=[vmem] * 2,
+        out_specs=(pl.BlockSpec(memory_space=pltpu.HBM),) * 2,
+        scratch_shapes=[dma, dma],
+        compiler_params=pltpu.CompilerParams(vmem_limit_bytes=2**20),
+    )(kernel_grads, outgoing)
     return kernel_grads[None], outgoing.reshape(1, H, W, C)
 
 

time: 52.6 us -> 51.5 us (0.979)
  local copies, waits for them, and re-layouts: 1.37 us -> 0 us
    unnamed x2 -> x0, local copies, waits for them, and re-layouts: 1.37 us -> none
    pallas_call x0 -> x1, Pallas kernels: none -> 0.77 us  [per_device(): pl.pallas_call(store, out_shape=(jax.ShapeDtypeStruct((ROWS, C), F32), ja...]
where the time goes in v4:
time: 51.5 us; the launch traced here: 51.4 us
  Pallas kernels  50.8 us (99%)
  between operations  0.64 us (1%)
    pallas_call x1, Pallas kernels, per_device(): pl.pallas_call(kernel, out_shape=(pltpu.VMEM((ROWS, C), F32), pltpu.VMEM(...  50 us

profile of v4, /device:TPU:1, one launch (start us, length us, event | category | flops | bytes accessed | tf_op | source)
XLA Modules:
  0.0 51.4 jit_solution(12300226570089140260)
XLA Ops:
  0.6 50.0 %shard_map.77 = (f32[144,256]{1,0:T(8,128)S(1)}, bf16[512,256]{1,0:T(8,128)(2,1)S(1)}) custom-call(bf16[4,512,256]{2,1,0:T(8,128)(2,1)} %bitcast.9, s32[4,512,256]{2,1,0:T(8,128)} %bitcast.7, bf16[512,256]{1,0:T(8,128)(2,1)} %bitcast.11, bf16[3,512,256]{2,1,0:T(8,128)(2,1)} %bitcast.10, bf16[2304,256]{1,0:T(8,128)(2,1)} %bitcast.8, f32[1,256]{1,0:T(1,128)} %sc_hbm.1), custom_call_target="tpu_custom_call" | custom-call | flops 4831838208 | bytes 6291456 | tf_op jit(solution)/shard_map/pallas_call | solution.py:487
  50.6 0.8 %shard_map.78 = (f32[144,256]{1,0:T(8,128)}, bf16[512,256]{1,0:T(8,128)(2,1)}) custom-call(f32[144,256]{1,0:T(8,128)S(1)} %get-tuple-element.6.kg_in, bf16[512,256]{1,0:T(8,128)(2,1)S(1)} %get-tuple-element.7.out_in), custom_call_target="tpu_custom_call" | custom-call | tf_op jit(solution)/shard_map/pallas_call | solution.py:544

commit v5 on v4

--- a/solution.py
+++ b/solution.py
@@ -17,7 +17,7 @@
 GRID = PX + 2 * LEAD * W
 SECTIONS, TILES, RING = 32, 16, 8
 ROWS = 9 * C // TILES
-PIECES = ((0, 80), (80, 64))
+PIECES = ((0, ROWS),)
 PLAN = {
     "F4+": (1, 4, 1, None), "F3+": (1, 3, 1, "F4+"), "F2+": (1, 2, 1, "F3+"), "F1+": (1, 1, 1, "F2+"),
     "F3-": (1, 3, -1, None), "F2-": (1, 2, -1, "F3-"), "F1-": (1, 1, -1, "F2-"), "F0": (1, 0, 0, None),
@@ -156,9 +156,20 @@
             p0_send.at[side], p0_recv.at[1 - side], s, beside(side),
         )
 
-    def mask_aside(side):
+    depth = (2, 1, 2, 1)
+    mask_at = (None, 0, 1, 3)
+
+    def mask_aside(t, side):
+        at = rows(mask_at[t], depth[t], 0)
         return to_tile(
-            edge.at[side], mh.at[1 - side], mh_send.at[side], mh_recv.at[1 - side], s, beside(side)
+            edge.at[side, at], mh.at[1 - side, at],
+            mh_send.at[t - 1, side], mh_recv.at[t - 1, 1 - side], s, beside(side),
+        )
+
+    def got_mask(t, side):
+        at = rows(mask_at[t], depth[t], 0)
+        pl.when(has_tile[side])(
+            lambda: local(edge.at[side, at], mh.at[side, at], mh_recv.at[t - 1, side]).wait()
         )
 
     def head_local(t, first, count, sem):
@@ -206,9 +217,6 @@
     def own_rows(t, first, count):
         grads = gb[t, rows(first, count), :].astype(F32)
         put(t, first, jnp.where(mv[t, rows(first, count, 0), :] != 0, grads * scales, 0.0))
-
-    depth = (2, 1, 2, 1)
-    mask_at = (None, 0, 1, 3)
 
     def beyond(t, side):
         count = depth[t]
@@ -308,7 +316,8 @@
 
         @pl.when(has_tile[side])
         def _(side=side):
-            mask_aside(side).start()
+            for t in range(1, T):
+                mask_aside(t, side).start()
 
             @pl.when(top)
             def _():
@@ -337,10 +346,8 @@
     x_load(0).wait()
     kernel_term(0)
     for side in range(2):
-        pl.when(has_tile[side])(
-            lambda side=side: local(edge.at[side], mh.at[side], mh_recv.at[side]).wait()
-        )
         got_end(1, side)
+        got_mask(1, side)
         own_rows(1, side * (H - 1), 1)
         beyond(1, side)
     end_parts(1)
@@ -361,6 +368,7 @@
         pl.when(has_tile[side])(
             lambda side=side: local(gin_hbm.at[rows(0, 2, 0)], far(2, 1 - side), gd_recv.at[side]).wait()
         )
+        got_mask(2, side)
         beyond(2, side)
     end_parts(2)
     x_load(2).wait()
@@ -377,6 +385,7 @@
     own_rows(last, 8, 7)
     for side in range(2):
         got_end(last, side)
+        got_mask(last, side)
         own_rows(last, side * (H - 1), 1)
         beyond(last, side)
 
@@ -412,7 +421,7 @@
         row = lax.broadcasted_iota(jnp.int32, (ROWS, C), 0) + at
         own = jnp.where(row < C, term(tap), term(jnp.minimum(tap + 1, 8)))
         sbuf[ORDER.index(name)] = (acc[piece(name, 0, True), :] + own).astype(BF16)
-        for part in range(2):
+        for part in range(len(PIECES)):
             message(name, part).start()
 
     def later_message(name, part):
@@ -431,12 +440,12 @@
     for name in ORDER[FIRST:]:
         if name == "F0":
             pl.when(z == 0)(lambda: pl.semaphore_wait(ready, 3))
-        for part in range(2):
+        for part in range(len(PIECES)):
             later_message(name, part)
         if name == "F1+":
             out_ref[...] = conv(last, [0], H)
 
-    for part in range(2):
+    for part in range(len(PIECES)):
         start, count = PIECES[part]
         at = pl.ds(start, count)
         total = acc[pl.ds(pl.multiple_of(j * ROWS + start, 16), count), :]
@@ -446,14 +455,15 @@
         kg_ref[at, :] = total * (1.0 / math.sqrt(T * TILES * PX))
 
     for name in ORDER:
-        for part in range(2):
+        for part in range(len(PIECES)):
             message(name, part).wait_send()
     for side in range(2):
 
         @pl.when(has_tile[side])
         def _(side=side):
             first_aside(side).wait_send()
-            mask_aside(side).wait_send()
+            for t in range(1, T):
+                mask_aside(t, side).wait_send()
             pl.when(sends)(lambda: pass_aside(side).wait_send())
 
             @pl.when(top)
@@ -521,10 +531,10 @@
             dma((T - 1, 2)),
             dma((2,)),
             dma((2,)),
-            dma((2,)),
-            dma((2,)),
-            dma((len(ORDER), 2)),
-            dma((len(ORDER), 2)),
+            dma((T - 1, 2)),
+            dma((T - 1, 2)),
+            dma((len(ORDER), len(PIECES))),
+            dma((len(ORDER), len(PIECES))),
             pltpu.SemaphoreType.REGULAR,
         ],
         compiler_params=pltpu.CompilerParams(

time: 51.5 us -> 51.4 us (level)
  no operation moved by 1% of the time
where the time goes in v5:
time: 51.4 us; the launch traced here: 51.2 us
  Pallas kernels  50.6 us (98%)
  between operations  0.64 us (1%)
    pallas_call x1, Pallas kernels, per_device(): pl.pallas_call(kernel, out_shape=(pltpu.VMEM((ROWS, C), F32), pltpu.VMEM(...  49.8 us

profile of v5, /device:TPU:1, one launch (start us, length us, event | category | flops | bytes accessed | tf_op | source)
XLA Modules:
  0.0 51.2 jit_solution(4426525575918735276)
XLA Ops:
  0.6 49.8 %shard_map.77 = (f32[144,256]{1,0:T(8,128)S(1)}, bf16[512,256]{1,0:T(8,128)(2,1)S(1)}) custom-call(bf16[4,512,256]{2,1,0:T(8,128)(2,1)} %bitcast.9, s32[4,512,256]{2,1,0:T(8,128)} %bitcast.7, bf16[512,256]{1,0:T(8,128)(2,1)} %bitcast.11, bf16[3,512,256]{2,1,0:T(8,128)(2,1)} %bitcast.10, bf16[2304,256]{1,0:T(8,128)(2,1)} %bitcast.8, f32[1,256]{1,0:T(1,128)} %sc_hbm.1), custom_call_target="tpu_custom_call" | custom-call | flops 4831838208 | bytes 6291456 | tf_op jit(solution)/shard_map/pallas_call | solution.py:497
  50.5 0.8 %shard_map.78 = (f32[144,256]{1,0:T(8,128)}, bf16[512,256]{1,0:T(8,128)(2,1)}) custom-call(f32[144,256]{1,0:T(8,128)S(1)} %get-tuple-element.6.kg_in, bf16[512,256]{1,0:T(8,128)(2,1)S(1)} %get-tuple-element.7.out_in), custom_call_target="tpu_custom_call" | custom-call | tf_op jit(solution)/shard_map/pallas_call | solution.py:554
